TPU v7x, 32 devices: a whole 2x2x4 slice. The times are simulated.
32 devices in a mesh: seq: 8 (over z, y), grp: 4 (over x, core).
Axes of the slice: x: 2, y: 2, z: 4, core: 2. Of those that a mesh axis runs over, the one named last changes fastest.
Arguments:
- q_nope: bfloat16 [128, 128, 128], P('seq', 'grp'), may hold values from -6 to 6
- q_rope: bfloat16 [128, 128, 64], P('seq', 'grp'), may hold values from -256 to 256
- cache: bfloat16 [8192, 576], P('seq'), may hold values from -6 to 6
- w_uk: bfloat16 [128, 65536], P('grp', 'seq'), may hold values from -0.5 to 0.5
- w_uv: bfloat16 [128, 65536], P('grp', 'seq'), may hold values from -0.25 to 0.25
- d_out: bfloat16 [128, 128, 128], P('seq', 'grp'), may hold values from -6 to 6
- sel: int32 [128, 32], P('seq'), may hold values from 0 to 63, as said below
- slot_blocks: int32 [8, 64], P('seq'), may hold values from 0 to 15, as said below
Outputs:
- attn_out: bfloat16 [128, 128, 128], P('seq', 'grp')
- d_q_nope: bfloat16 [128, 128, 128], P('seq', 'grp')
- d_q_rope: bfloat16 [128, 128, 64], P('seq', 'grp')
- d_cache: float32 [8192, 576], P('seq')
Inputs may be any that keep to these rules, and one draw needn't show every extreme that they name: `sel`: each row names 32 different places; place s stands for the block that the row's device asks of device s // 8. `slot_blocks`: entry [r, s] is the index among device s // 8's own blocks of the block that device r asks for in place s; the 8 entries of a row toward one device differ.
All inputs are finite; a program needn't handle non-finite values.
Results may differ from a plain program's by a relative error of at most 0.015.
Values may be sent and summed in bfloat16 or wider, within the bound.
No kernel may reach another device: no remote copies, remote signals or barrier semaphores. Data moves between devices by JAX's collectives and lax.ppermute only.
A program may use at most 128 MiB of HBM per device.

v0:
```python
import math

import jax
import jax.numpy as jnp
from jax import lax
from jax.sharding import PartitionSpec as P

BLOCK_LEN = 64


def local(q_nope, q_rope, cache, w_uk, w_uv, d_out, sel, slot_blocks):
    peers = lax.axis_size("seq")
    queries, heads, nope = q_nope.shape
    rope = q_rope.shape[2]
    width = cache.shape[1]
    latent = width - rope
    value = d_out.shape[2]
    slot_total = slot_blocks.shape[1]
    per_peer = slot_total // peers
    own_blocks = cache.shape[0] // BLOCK_LEN
    scale = 1.0 / math.sqrt(nope + rope)
    gathered_k, gathered_v = (
        lax.all_gather(w_uk, "seq", axis=1, tiled=True),
        lax.all_gather(w_uv, "seq", axis=1, tiled=True),
    )
    weight_k = gathered_k.reshape(heads, nope, latent)
    weight_v = gathered_v.reshape(heads, latent, value)
    wanted = slot_blocks.reshape(peers, per_peer)
    asked = lax.all_to_all(wanted, "seq", split_axis=0, concat_axis=0, tiled=True)
    blocks = cache.reshape(own_blocks, BLOCK_LEN, width)
    arrived = lax.all_to_all(blocks[asked], "seq", split_axis=0, concat_axis=0, tiled=True)
    keys = arrived.reshape(slot_total * BLOCK_LEN, width)
    keys_lat = keys[:, :latent]
    q_lat = jnp.einsum("qhn,hnl->qhl", q_nope, weight_k, preferred_element_type=jnp.float32).astype(
        jnp.bfloat16
    )
    qfull = jnp.concatenate([q_lat, q_rope], axis=-1)
    chosen = jnp.any(
        sel[:, :, None] == jnp.arange(slot_total, dtype=jnp.int32)[None, None, :], axis=1
    )
    live = jnp.repeat(chosen, BLOCK_LEN, axis=1)[:, None, :]
    score = jnp.einsum("qhc,tc->qht", qfull, keys, preferred_element_type=jnp.float32) * scale
    score = jnp.where(live, score, -jnp.inf)
    prob = jax.nn.softmax(score, axis=-1)
    prob_low = prob.astype(jnp.bfloat16)
    olat = jnp.einsum("qht,tl->qhl", prob_low, keys_lat, preferred_element_type=jnp.float32).astype(
        jnp.bfloat16
    )
    attn_out = jnp.einsum(
        "qhl,hlv->qhv", olat, weight_v, preferred_element_type=jnp.float32
    ).astype(jnp.bfloat16)
    d_olat = jnp.einsum("qhv,hlv->qhl", d_out, weight_v, preferred_element_type=jnp.float32).astype(
        jnp.bfloat16
    )
    dprob = jnp.einsum("qhl,tl->qht", d_olat, keys_lat, preferred_element_type=jnp.float32)
    delta = jnp.sum(prob * dprob, axis=-1, keepdims=True)
    dscore = (prob * (dprob - delta) * scale).astype(jnp.bfloat16)
    dquery = jnp.einsum("qht,tc->qhc", dscore, keys, preferred_element_type=jnp.float32)
    d_q_rope = dquery[:, :, latent:].astype(jnp.bfloat16)
    d_qlat = dquery[:, :, :latent].astype(jnp.bfloat16)
    d_q_nope = jnp.einsum(
        "qhl,hnl->qhn", d_qlat, weight_k, preferred_element_type=jnp.float32
    ).astype(jnp.bfloat16)
    value_part = jnp.einsum("qht,qhl->tl", prob_low, d_olat, preferred_element_type=jnp.float32)
    dkeys = jnp.einsum("qht,qhc->tc", dscore, qfull, preferred_element_type=jnp.float32)
    dkeys = dkeys + jnp.pad(value_part, ((0, 0), (0, rope)))
    one_hot = (
        asked.reshape(-1)[:, None] == jnp.arange(own_blocks, dtype=jnp.int32)[None, :]
    ).astype(jnp.float32)
    returned = lax.all_to_all(
        dkeys.reshape(peers, per_peer, BLOCK_LEN * width).astype(jnp.bfloat16),
        "seq",
        split_axis=0,
        concat_axis=0,
        tiled=True,
    ).astype(jnp.float32)
    local_grad = jnp.dot(
        one_hot.T,
        returned.reshape(peers * per_peer, BLOCK_LEN * width),
        precision=lax.Precision.HIGHEST,
    )
    d_cache = (
        lax.psum(local_grad.astype(jnp.bfloat16), "grp")
        .astype(jnp.float32)
        .reshape(own_blocks * BLOCK_LEN, width)
    )
    return (attn_out, d_q_nope, d_q_rope, d_cache)


def solution(mesh):
    return jax.shard_map(
        local,
        mesh=mesh,
        in_specs=(
            P("seq", "grp", None),
            P("seq", "grp", None),
            P("seq", None),
            P("grp", "seq"),
            P("grp", "seq"),
            P("seq", "grp", None),
            P("seq", None),
            P("seq", None),
        ),
        out_specs=(
            P("seq", "grp", None),
            P("seq", "grp", None),
            P("seq", "grp", None),
            P("seq", None),
        ),
        check_vma=False,
    )
```

profile of v0, /device:TPU:0, one launch (start us, length us, event | category | flops | bytes accessed | tf_op | source)
XLA Modules:
  0.0 481.0 jit_solution(9508205699265830876)
XLA Ops:
  7.2 0.0 all-gather.3.cloned.1.call-start
  7.2 0.7 all-gather.3.cloned.1.call-update
  7.9 0.5 broadcast.46
  8.4 1.3 reduce.6
  9.7 0.7 all_to_all.14
  10.4 7.3 %all-to-all-start = ((s32[8,1,8]{2,1,0:T(1,128)}), s32[8,1,8]{2,1,0:T(1,128)S(1)}, u32[]{:S(2)}, u32[]{:S(2)}) async-start(s32[8,1,8]{2,1,0:T(1,128)} %bitcast.2), calls=%async_computation | async-start | bytes 8192 | tf_op jit(solution)/shard_map/all_to_all | solution.py:29
  17.7 1.7 copy.58
  19.4 4.7 all-to-all-done
  24.1 0.1 reshape.79
  24.2 3.5 gather_fusion
  27.7 4.8 %all-to-all-start.1 = ((bf16[8,8,64,576]{3,2,1,0:T(8,128)(2,1)}), bf16[8,8,64,576]{3,2,1,0:T(8,128)(2,1)}, u32[]{:S(2)}, u32[]{:S(2)}) async-start(bf16[8,8,64,576]{3,2,1,0:T(8,128)(2,1)} %bitcast.48), calls=%async_computation.1 | async-start | bytes 10485760 | tf_op jit(solution)/shard_map/all_to_all | solution.py:31
  32.5 0.0 all-gather.5.cloned.1.call-start
  32.6 0.7 all-gather.5.cloned.1.call-update
  33.3 0.2 fusion.37
  33.4 0.2 broadcast_in_dim.24
  33.6 0.2 broadcast_in_dim.25
  33.9 0.1 copy.57
  34.0 140.5 %all-gather.3.cloned.1.call-done = bf16[32,65536]{1,0:T(8,128)(2,1)} async-done(((bf16[32,8192]{1,0:T(8,128)(2,1)}), bf16[32,65536]{1,0:T(8,128)(2,1)}) %all-gather.3.cloned.1.call-update) | async-done | bytes 4194320 | tf_op jit(solution)/shard_map/all_gather | solution.py:23
  174.5 5.7 %copy.77 = bf16[4,8,128,512]{3,2,1,0:T(8,128)(2,1)} copy(bf16[4,8,128,512]{3,1,2,0:T(8,128)(2,1)} %bitcast.49) | data formatting | bytes 8388608
  180.2 69.0 %all-gather.5.cloned.1.call-done = bf16[32,65536]{1,0:T(8,128)(2,1)} async-done(((bf16[32,8192]{1,0:T(8,128)(2,1)}), bf16[32,65536]{1,0:T(8,128)(2,1)}) %all-gather.5.cloned.1.call-update) | async-done | bytes 4194320 | tf_op jit(solution)/shard_map/all_gather | solution.py:24
  249.2 3.3 copy.78
  252.6 0.1 copy-done.2
  252.7 0.6 fusion.27
  253.3 0.1 pad_maximum_fusion
  253.4 1.1 copy-done.4
  254.5 1.2 fusion.26
  255.7 7.9 %fusion.11 = f32[16,32,4096]{2,1,0:T(8,128)} fusion(bf16[4096,576]{1,0:T(8,128)(2,1)} %bitcast.5, bf16[16,32,512]{2,0,1:T(8,128)(2,1)S(1)} %fusion.26), kind=kOutput, calls=%fused_computation.19 | convolution fusion | flops 2147483648 | bytes 13107200 | tf_op jit(solution)/shard_map/qhl,tl->qht/dot_general | solution.py:55
  263.6 10.6 %fusion.47 = (f32[16,32]{1,0:T(8,128)S(1)}, f32[16,32,4096]{2,1,0:T(8,128)}) fusion(pred[16,4096]{1,0:T(8,128)(4,1)S(1)} %broadcast_in_dim.25, bf16[4096,576,1]{1,0,2:T(8,128)(2,1)} %bitcast.6, bf16[16,32,576]{2,0,1:T(8,128)(2,1)S(1)} %pad_maximum_fusion), kind=kOutput, calls=%fused_computation.56 | convolution fusion | flops 2424311808 | bytes 13764608 | tf_op jit(solution)/shard_map/sub | solution.py:44
  274.2 9.4 %convolution_bitcast_fusion = f32[4096,512]{0,1:T(8,128)} fusion(bf16[16,32,512]{2,0,1:T(8,128)(2,1)S(1)} %fusion.26, f32[16,32,4096]{2,1,0:T(8,128)} %get-tuple-element.21, f32[16,32]{1,0:T(8,128)S(1)} %get-tuple-element.20), kind=kOutput, calls=%fused_computation.12 | convolution fusion | flops 2151677952 | bytes 17303552 | tf_op jit(solution)/shard_map/qht,qhl->tl/dot_general | solution.py:64
  283.6 18.7 %fusion.2 = bf16[4096,576]{0,1:T(8,128)(2,1)} fusion(f32[4096,512]{0,1:T(8,128)} %convolution_bitcast_fusion, f32[16,32,4096]{2,1,0:T(8,128)} %fusion.11, bf16[16,32,576]{2,0,1:T(8,128)(2,1)S(1)} %pad_maximum_fusion, f32[16,32,4096]{2,1,0:T(8,128)} %get-tuple-element.21, f32[16,32]{1,0:T(8,128)S(1)} %get-tuple-element.20), kind=kOutput, calls=%fused_computation.5 | convolution fusion | flops 2435322368 | bytes 30476288 | tf_op jit(solution)/shard_map/qht,qhc->tc/dot_general | solution.py:65
  302.4 7.6 %copy.69 = bf16[4096,576]{1,0:T(8,128)(2,1)} copy(bf16[4096,576]{0,1:T(8,128)(2,1)} %fusion.2) | data formatting | bytes 9437184 | tf_op jit(solution)/shard_map/convert_element_type | solution.py:71
  310.0 9.9 %convert_element_type.61 = bf16[8,8,36864]{2,1,0:T(8,128)(2,1)} reshape(bf16[4096,576]{1,0:T(8,128)(2,1)} %copy.69) | data formatting | bytes 9437184 | tf_op jit(solution)/shard_map/convert_element_type | solution.py:71
  319.9 4.6 all-to-all-start.2
  324.5 0.3 all-reduce.3.cloned.1.call-start
  324.8 0.7 reduce.7
  325.4 0.1 eq.31
  325.5 14.5 %fusion.20 = bf16[16,32,576]{2,1,0:T(8,128)(2,1)S(1)} fusion(bf16[4096,576,1]{1,0,2:T(8,128)(2,1)} %bitcast.6, f32[16,32,4096]{2,1,0:T(8,128)} %fusion.11, f32[16,32,4096]{2,1,0:T(8,128)} %get-tuple-element.21, f32[16,32]{1,0:T(8,128)S(1)} %get-tuple-element.20), kind=kOutput, calls=%fused_computation.24 | convolution fusion | flops 2430898688 | bytes 22087680 | tf_op jit(solution)/shard_map/qht,tc->qhc/dot_general | solution.py:58
  340.1 0.7 slice.18
  340.8 6.9 %fusion.23 = bf16[16,32,512]{2,1,0:T(8,128)(2,1)S(1)} fusion(bf16[4096,576]{1,0:T(8,128)(2,1)} %bitcast.5, f32[16,32,4096]{2,1,0:T(8,128)} %get-tuple-element.21, f32[16,32]{1,0:T(8,128)S(1)} %get-tuple-element.20), kind=kOutput, calls=%fused_computation.25 | convolution fusion | flops 2151940096 | bytes 13109248 | tf_op jit(solution)/shard_map/qht,tl->qhl/dot_general | solution.py:46
  347.8 80.2 %all-to-all-done.2 = bf16[8,8,36864]{2,1,0:T(8,128)(2,1)} async-done(((bf16[8,8,36864]{2,1,0:T(8,128)(2,1)}), bf16[8,8,36864]{2,1,0:T(8,128)(2,1)}, u32[]{:S(2)}, u32[]{:S(2)}) %all-to-all-start.2) | async-done | bytes 4718624 | tf_op jit(solution)/shard_map/all_to_all | solution.py:70
  428.0 3.2 convolution_convert_fusion
  431.2 2.5 reshape.75
  433.7 3.2 fusion.28
  436.9 0.7 copy.70
  437.6 1.2 fusion.29
  438.8 0.7 copy.71
  439.5 32.2 %all-reduce.3.cloned.1.call-done = bf16[1024,576]{1,0:T(8,128)(2,1)} async-done(((bf16[1024,576]{1,0:T(8,128)(2,1)}), bf16[1024,576]{1,0:T(8,128)(2,1)}) %all-reduce.3.cloned.1.call-update) | async-done | bytes 1179664 | tf_op jit(solution)/shard_map/psum | solution.py:83
  471.8 2.7 copy.72
  (22 shorter events, 0.1 us)
Async XLA Ops:
  7.2 247.4 %copy-start = (bf16[16,32,128]{2,1,0:T(8,128)(2,1)S(1)}, bf16[16,32,128]{2,1,0:T(8,128)(2,1)}, u32[]{:S(2)}) copy-start(bf16[16,32,128]{2,1,0:T(8,128)(2,1)} %param.13) | copy-start | bytes 393220
  7.2 167.3 %all-gather.3.cloned.1.call-start = ((), (), s32[]{:S(2)}) async-start(), calls=%async_computation.3 | async-start | bytes 4718592 | tf_op jit(solution)/shard_map/all_gather | solution.py:23
  10.4 13.7 %all-to-all-start = ((s32[8,1,8]{2,1,0:T(1,128)}), s32[8,1,8]{2,1,0:T(1,128)S(1)}, u32[]{:S(2)}, u32[]{:S(2)}) async-start(s32[8,1,8]{2,1,0:T(1,128)} %bitcast.2), calls=%async_computation | async-start | bytes 8192 | tf_op jit(solution)/shard_map/all_to_all | solution.py:29
  27.7 5.6 %copy-start.8 = (s32[16,32]{1,0:T(8,128)S(1)}, s32[16,32]{1,0:T(8,128)}, u32[]{:S(2)}) copy-start(s32[16,32]{1,0:T(8,128)} %param.14) | copy-start | bytes 6148
  27.7 6.2 %copy-start.7 = (bf16[16,32,64]{2,1,0:T(8,128)(2,1)S(1)}, bf16[16,32,64]{2,1,0:T(8,128)(2,1)}, u32[]{:S(2)}) copy-start(bf16[16,32,64]{2,1,0:T(8,128)(2,1)} %param.9) | copy-start | bytes 196612
  27.7 228.1 %all-to-all-start.1 = ((bf16[8,8,64,576]{3,2,1,0:T(8,128)(2,1)}), bf16[8,8,64,576]{3,2,1,0:T(8,128)(2,1)}, u32[]{:S(2)}, u32[]{:S(2)}) async-start(bf16[8,8,64,576]{3,2,1,0:T(8,128)(2,1)} %bitcast.48), calls=%async_computation.1 | async-start | bytes 10485760 | tf_op jit(solution)/shard_map/all_to_all | solution.py:31
  32.5 216.7 %all-gather.5.cloned.1.call-start = ((), (), s32[]{:S(2)}) async-start(), calls=%async_computation.4 | async-start | bytes 4718592 | tf_op jit(solution)/shard_map/all_gather | solution.py:24
  180.2 72.4 %copy-start.6 = (bf16[16,32,128]{2,1,0:T(8,128)(2,1)S(1)}, bf16[16,32,128]{2,1,0:T(8,128)(2,1)}, u32[]{:S(2)}) copy-start(bf16[16,32,128]{2,1,0:T(8,128)(2,1)} %param.8) | copy-start | bytes 393220
  249.2 3.4 copy-start.2
  252.6 2.0 copy-start.4
  319.9 108.1 %all-to-all-start.2 = ((bf16[8,8,36864]{2,1,0:T(8,128)(2,1)}), bf16[8,8,36864]{2,1,0:T(8,128)(2,1)}, u32[]{:S(2)}, u32[]{:S(2)}) async-start(bf16[8,8,36864]{2,1,0:T(8,128)(2,1)} %convert_element_type.61), calls=%async_computation.2 | async-start | bytes 9437184 | tf_op jit(solution)/shard_map/all_to_all | solution.py:70
  324.5 147.3 %all-reduce.3.cloned.1.call-start = ((), (), s32[]{:S(2)}) async-start(), calls=%async_computation.5 | async-start | bytes 2621440 | tf_op jit(solution)/shard_map/psum | solution.py:83
  340.0 7.7 %copy-start.5 = (bf16[16,32,576]{2,1,0:T(8,128)(2,1)}, bf16[16,32,576]{2,1,0:T(8,128)(2,1)S(1)}, u32[]{:S(2)}) copy-start(bf16[16,32,576]{2,1,0:T(8,128)(2,1)S(1)} %fusion.20) | copy-start | bytes 1769476
  431.2 6.4 %slice-start = ((bf16[16,32,576]{2,1,0:T(8,128)(2,1)}), bf16[16,32,512]{2,1,0:T(8,128)(2,1)S(1)}, s32[]{:S(2)}) async-start(bf16[16,32,576]{2,1,0:T(8,128)(2,1)} %copy-done.5), calls=%async_computation.6 | async-start | bytes 1048576 | tf_op jit(solution)/shard_map/slice | solution.py:60
  433.7 3.9 copy-start.3
  433.7 40.8 %copy-start.1 = (bf16[16,32,128]{2,1,0:T(8,128)(2,1)S(1)}, bf16[16,32,128]{2,1,0:T(8,128)(2,1)}, u32[]{:S(2)}) copy-start(bf16[16,32,128]{2,1,0:T(8,128)(2,1)} %param.13) | copy-start | bytes 393220
Sparse Core Ops, SparseCore 0:
  10.2 164.2 all-gather.2
  176.7 72.5 all-gather.4
  433.8 37.9 all-reduce.2
where the time goes:
time: 482 us; the launch traced here: 481 us
  waiting for transfers between devices  328 us (68%)
  matrix products  77.5 us (16%)
  local copies, waits for them, and re-layouts  42.2 us (9%)
  starting transfers between devices  17.1 us (4%)
  between operations  13.9 us (3%)
    all_gather x1, waiting for transfers between devices, local(): lax.all_gather(w_uk, 'seq', axis=1, tiled=True)  141 us
    all_to_all x1, waiting for transfers between devices, local(): lax.all_to_all(dkeys.reshape(peers, per_peer, BLOCK_LEN * width).astype(j...  80.2 us
    all_gather x1, waiting for transfers between devices, local(): lax.all_gather(w_uv, 'seq', axis=1, tiled=True)  69 us
    psum x1, waiting for transfers between devices, local(): lax.psum(local_grad.astype(jnp.bfloat16), 'grp').astype(jnp.float32)  32.2 us
    dot_general x1, matrix products, local(): jnp.einsum('qht,qhc->tc', dscore, qfull, preferred_element_type=jnp.float32)  18.7 us
    convert_element_type x2, local copies, waits for them, and re-layouts, local(): dkeys.reshape(peers, per_peer, BLOCK_LEN * width).astype(jnp.bfloat16)  17.5 us
    unnamed x26, local copies, waits for them, and re-layouts  16.7 us
    dot_general x1, matrix products, local(): jnp.einsum('qht,tc->qhc', dscore, keys, preferred_element_type=jnp.float32)  14.5 us
  transfers between devices with their start and end apart: 6, of which 5 were waited for; matrix products, arithmetic and copies ran while one was open for 10% of the time, Pallas kernels for 0%

commit v1 on v0

v1 whole, which is shorter than its diff:
```python
import functools
import math

import jax
import jax.numpy as jnp
from jax import lax
from jax.experimental import pallas as pl
from jax.experimental.pallas import tpu as pltpu
from jax.sharding import PartitionSpec as P

BLOCK_LEN = 64
LANES = 128
HIDDEN = -1e30
VMEM = pl.BlockSpec(memory_space=pltpu.VMEM)
SMEM = pl.BlockSpec(memory_space=pltpu.SMEM)
F32 = jnp.float32
BF16 = jnp.bfloat16


def params(mib):
    return pltpu.CompilerParams(vmem_limit_bytes=mib * 2**20)


def nt(a, b):
    return lax.dot_general(a, b, (((1,), (1,)), ((), ())), preferred_element_type=F32)


def nn(a, b):
    return lax.dot_general(a, b, (((1,), (0,)), ((), ())), preferred_element_type=F32)


def tn(a, b):
    return lax.dot_general(a, b, (((0,), (0,)), ((), ())), preferred_element_type=F32)


def seq_swap(x):
    return lax.all_to_all(x, "seq", split_axis=0, concat_axis=0, tiled=True)


def grp_swap(x, bit):
    n = lax.axis_size("grp")
    return lax.ppermute(x, "grp", [(i, i ^ bit) for i in range(n)])


def weight_k_of(pack, head, uk_rows, tiles):
    rows = uk_rows // tiles
    peers = pack.shape[0]
    cols = []
    for t in range(tiles):
        cols.append(
            jnp.concatenate(
                [pack[r, head, t * rows : (t + 1) * rows, :] for r in range(peers)], axis=0
            )
        )
    return jnp.concatenate(cols, axis=1)


def stacked(pack, head, start, rows):
    peers = pack.shape[0]
    return jnp.concatenate([pack[r, head, start : start + rows, :] for r in range(peers)], axis=0)


def expand_kernel(sizes, pack, out):
    uk_rows, uv_rows, queries, tiles, latent = sizes
    peers, heads = pack.shape[0], pack.shape[1]
    for h in range(heads):
        wk = weight_k_of(pack, h, uk_rows, tiles)
        wv = stacked(pack, h, uk_rows, uv_rows)
        qn = stacked(pack, h, uk_rows + uv_rows, queries)
        do = stacked(pack, h, uk_rows + uv_rows + queries, queries)
        q_lat = nn(qn, wk).astype(BF16)
        d_olat = nt(do, wv).astype(BF16)
        for r in range(peers):
            out[r, h, :, :latent] = q_lat[r * queries : (r + 1) * queries]
            out[r, h, :, latent:] = d_olat[r * queries : (r + 1) * queries]


def reduce_kernel(sizes, pack, lat, out):
    uk_rows, uv_rows, queries, tiles, latent = sizes
    peers, heads = pack.shape[0], pack.shape[1]
    for h in range(heads):
        wk = weight_k_of(pack, h, uk_rows, tiles)
        wv = stacked(pack, h, uk_rows, uv_rows)
        both = jnp.concatenate([lat[r, h] for r in range(peers)], axis=0)
        attn = nn(both[:, :latent], wv).astype(BF16)
        dqn = nt(both[:, latent:], wk).astype(BF16)
        for r in range(peers):
            out[r, h, :, : attn.shape[1]] = attn[r * queries : (r + 1) * queries]
            out[r, h, :, attn.shape[1] :] = dqn[r * queries : (r + 1) * queries]


def attend_kernel(scale, qd, rope, bias, *refs):
    parts = 4
    keys, refs = refs[:parts], refs[parts:]
    out, d_rope, refs = refs[0], refs[1], refs[2:]
    dkeys, refs = refs[:parts], refs[parts:]
    qf, cat, sc, dp, o_acc, q_acc = refs
    rows, width = qf.shape
    slots, part_len, _ = keys[0].shape
    latent = width - rope.shape[1]
    step = min(slots, 32)
    tokens = step * part_len
    qf[:, :latent] = qd[:, :latent]
    qf[:, latent:] = rope[...]
    cat[:rows] = qd[:, :latent]
    cat[rows:] = qd[:, latent:]
    chunks = [(p, c) for p in range(parts) for c in range(0, slots, step)]
    scale2 = scale * math.log2(math.e)

    top = jnp.full((1, rows), -jnp.inf, F32)
    for i, (p, c) in enumerate(chunks):
        k = keys[p][c : c + step].reshape(tokens, width)
        s = nt(k, qf[...]) * scale2
        b = jnp.broadcast_to(bias[c : c + step][:, None, :], (step, part_len, rows))
        s = s + b.reshape(tokens, rows)
        sc[pl.ds(i * tokens, tokens), :] = s
        dp[pl.ds(i * tokens, tokens), :] = nt(k[:, :latent], cat[rows:])
        top = jnp.maximum(top, jnp.max(s, axis=0, keepdims=True))

    total = jnp.zeros((1, rows), F32)
    inner = jnp.zeros((1, rows), F32)
    for i in range(len(chunks)):
        e = jnp.exp2(sc[pl.ds(i * tokens, tokens), :] - top)
        sc[pl.ds(i * tokens, tokens), :] = e
        total = total + jnp.sum(e, axis=0, keepdims=True)
        inner = inner + jnp.sum(e * dp[pl.ds(i * tokens, tokens), :], axis=0, keepdims=True)
    inv = 1.0 / total
    delta = inner * inv

    for i, (p, c) in enumerate(chunks):
        k = keys[p][c : c + step].reshape(tokens, width)
        prob = sc[pl.ds(i * tokens, tokens), :] * inv
        pb = prob.astype(BF16)
        ds = (prob * (dp[pl.ds(i * tokens, tokens), :] - delta) * scale).astype(BF16)
        o_part = tn(k[:, :latent], pb)
        q_part = tn(k, ds)
        if i == 0:
            o_acc[...] = o_part
            q_acc[...] = q_part
        else:
            o_acc[...] += o_part
            q_acc[...] += q_part
        both = jnp.concatenate([ds, pb], axis=1)
        dkeys[p][c : c + step, :, :latent] = (
            nn(both, cat[...]).astype(BF16).reshape(step, part_len, latent)
        )
        dkeys[p][c : c + step, :, latent:] = (
            nn(ds, rope[...]).astype(BF16).reshape(step, part_len, width - latent)
        )

    out[:, :latent] = o_acc[...].T.astype(BF16)
    out[:, latent:] = q_acc[:latent].T.astype(BF16)
    d_rope[...] = q_acc[latent:].T.astype(BF16)


def attend(scale, qd, rope, bias, keys):
    rows = qd.shape[0]
    slots, part_len, width = keys[0].shape
    latent = width - rope.shape[1]
    tokens = len(keys) * slots * part_len
    outs = pl.pallas_call(
        functools.partial(attend_kernel, scale),
        out_shape=[
            jax.ShapeDtypeStruct((rows, 2 * latent), BF16),
            jax.ShapeDtypeStruct(rope.shape, BF16),
        ]
        + [jax.ShapeDtypeStruct(k.shape, BF16) for k in keys],
        in_specs=[VMEM] * (3 + len(keys)),
        out_specs=[VMEM] * (2 + len(keys)),
        scratch_shapes=[
            pltpu.VMEM((rows, width), BF16),
            pltpu.VMEM((2 * rows, latent), BF16),
            pltpu.VMEM((tokens, rows), F32),
            pltpu.VMEM((tokens, rows), F32),
            pltpu.VMEM((latent, rows), F32),
            pltpu.VMEM((width, rows), F32),
        ],
        compiler_params=params(56),
        name="attend",
    )(qd, rope, bias, *keys)
    return outs[0], outs[1], outs[2:]


def scatter_kernel(asked, got, out, acc):
    acc[...] = jnp.zeros_like(acc)
    for s in range(got.shape[0]):
        b = asked[s]
        acc[b] = acc[b] + got[s].astype(F32)
    out[...] = acc[...].astype(BF16)


def assemble_kernel(place, y0, y1, y2, y3, out):
    for k, y in enumerate((y0, y1, y2, y3)):
        out[:, place[k]] = y[...].astype(F32)


def local(q_nope, q_rope, cache, w_uk, w_uv, d_out, sel, slot_blocks):
    peers = lax.axis_size("seq")
    groups = lax.axis_size("grp")
    me = lax.axis_index("grp")
    queries, heads, nope = q_nope.shape
    rope = q_rope.shape[2]
    width = cache.shape[1]
    latent = width - rope
    value = d_out.shape[2]
    slot_total = slot_blocks.shape[1]
    per_peer = slot_total // peers
    own_blocks = cache.shape[0] // BLOCK_LEN
    part_len = BLOCK_LEN // groups
    rows = heads * queries
    scale = 1.0 / math.sqrt(nope + rope)

    asked = seq_swap(slot_blocks.reshape(peers, per_peer)).reshape(-1)
    pieces = cache.reshape(own_blocks * groups, part_len, width)
    mine = pieces[asked * groups + me]
    qn = q_nope.transpose(1, 0, 2)
    do = d_out.transpose(1, 0, 2)
    head_form = heads % peers == 0
    if head_form:
        tiles = latent // LANES
        n_rows = w_uk.shape[1] // latent
        uv_rows = w_uv.shape[1] // value
        uk = w_uk.reshape(heads, n_rows, tiles, LANES).transpose(0, 2, 1, 3)
        pack = jnp.concatenate(
            [uk.reshape(heads, n_rows * tiles, LANES), w_uv.reshape(heads, uv_rows, value), qn, do],
            axis=1,
        )
        pack = seq_swap(pack).reshape(peers, heads // peers, -1, LANES)
        sizes = (n_rows * tiles, uv_rows, queries, tiles, latent)
        lat = pl.pallas_call(
            functools.partial(expand_kernel, sizes),
            out_shape=jax.ShapeDtypeStruct((peers, heads // peers, queries, 2 * latent), BF16),
            in_specs=[VMEM],
            out_specs=VMEM,
            compiler_params=params(32),
            name="expand",
        )(pack)
        qd = seq_swap(lat).reshape(rows, 2 * latent)
    else:
        weight_k = lax.all_gather(w_uk, "seq", axis=1, tiled=True).reshape(heads, nope, latent)
        weight_v = lax.all_gather(w_uv, "seq", axis=1, tiled=True).reshape(heads, latent, value)
        q_lat = jnp.einsum("hqn,hnl->hql", qn, weight_k, preferred_element_type=F32).astype(BF16)
        d_olat = jnp.einsum("hqv,hlv->hql", do, weight_v, preferred_element_type=F32).astype(BF16)
        qd = jnp.concatenate([q_lat, d_olat], axis=-1).reshape(rows, 2 * latent)

    k0 = seq_swap(mine.reshape(peers, per_peer * part_len, width)).reshape(
        slot_total, part_len, width
    )
    k2 = grp_swap(k0, 2)
    k1 = grp_swap(k0, 1)
    k3 = grp_swap(k2, 1)

    chosen = jnp.any(
        sel[None, :, :] == jnp.arange(slot_total, dtype=jnp.int32)[:, None, None], axis=2
    )
    bias = jnp.where(chosen, 0.0, HIDDEN).astype(F32)
    bias = jnp.broadcast_to(bias[:, None, :], (slot_total, heads, queries)).reshape(
        slot_total, rows
    )
    rope_rows = q_rope.transpose(1, 0, 2).reshape(rows, rope)
    lat, d_rope, dk = attend(scale, qd, rope_rows, bias, (k0, k1, k2, k3))

    a2 = (dk[2].astype(F32) + grp_swap(dk[3], 1).astype(F32)).astype(BF16)
    a0 = (dk[0].astype(F32) + grp_swap(dk[1], 1).astype(F32)).astype(BF16)
    a0 = (a0.astype(F32) + grp_swap(a2, 2).astype(F32)).astype(BF16)
    got = seq_swap(a0.reshape(peers, per_peer * part_len, width)).reshape(
        slot_total, part_len, width
    )

    if head_form:
        lat = seq_swap(lat.reshape(peers, heads // peers, queries, 2 * latent))
        res = pl.pallas_call(
            functools.partial(reduce_kernel, sizes),
            out_shape=jax.ShapeDtypeStruct((peers, heads // peers, queries, value + nope), BF16),
            in_specs=[VMEM, VMEM],
            out_specs=VMEM,
            compiler_params=params(32),
            name="reduce",
        )(pack, lat)
        res = seq_swap(res).reshape(heads, queries, value + nope)
        attn_out, d_q_nope = res[:, :, :value], res[:, :, value:]
    else:
        lat = lat.reshape(heads, queries, 2 * latent)
        attn_out = jnp.einsum(
            "hql,hlv->hqv", lat[:, :, :latent], weight_v, preferred_element_type=F32
        ).astype(BF16)
        d_q_nope = jnp.einsum(
            "hql,hnl->hqn", lat[:, :, latent:], weight_k, preferred_element_type=F32
        ).astype(BF16)

    y0 = pl.pallas_call(
        scatter_kernel,
        out_shape=jax.ShapeDtypeStruct((own_blocks, part_len, width), BF16),
        in_specs=[SMEM, VMEM],
        out_specs=VMEM,
        scratch_shapes=[pltpu.VMEM((own_blocks, part_len, width), F32)],
        compiler_params=params(16),
        name="scatter",
    )(asked, got)
    y2 = grp_swap(y0, 2)
    y1 = grp_swap(y0, 1)
    y3 = grp_swap(y2, 1)
    place = jnp.bitwise_xor(me, jnp.arange(4, dtype=jnp.int32))
    d_cache = pl.pallas_call(
        assemble_kernel,
        out_shape=jax.ShapeDtypeStruct((own_blocks, groups, part_len, width), F32),
        in_specs=[SMEM, VMEM, VMEM, VMEM, VMEM],
        out_specs=VMEM,
        compiler_params=params(16),
        name="assemble",
    )(place, y0, y1, y2, y3).reshape(own_blocks * BLOCK_LEN, width)
    return (
        attn_out.transpose(1, 0, 2),
        d_q_nope.transpose(1, 0, 2),
        d_rope.reshape(heads, queries, rope).transpose(1, 0, 2),
        d_cache,
    )


def solution(mesh):
    return jax.shard_map(
        local,
        mesh=mesh,
        in_specs=(
            P("seq", "grp", None),
            P("seq", "grp", None),
            P("seq", None),
            P("grp", "seq"),
            P("grp", "seq"),
            P("seq", "grp", None),
            P("seq", None),
            P("seq", None),
        ),
        out_specs=(
            P("seq", "grp", None),
            P("seq", "grp", None),
            P("seq", "grp", None),
            P("seq", None),
        ),
        check_vma=False,
    )
```

time: 482 us -> 241 us (0.50)
  waiting for transfers between devices: 328 us -> 145 us
  matrix products: 77.5 us -> 0 us
  Pallas kernels: 0 us -> 29 us
  local copies, waits for them, and re-layouts: 42.2 us -> 20.6 us
  starting transfers between devices: 17.1 us -> 37.8 us
  between operations: 13.9 us -> 0.88 us
    all_gather x2 -> x0, waiting for transfers between devices: 210 us -> none  [the longest x1 141 us: local(): lax.all_gather(w_uk, 'seq', axis=1, tiled=True)]
    dot_general x10 -> x0, matrix products: 66.8 us -> none  [the longest x1 18.7 us: local(): jnp.einsum('qht,qhc->tc', dscore, qfull, preferred_element_type=jnp.float32)]
    ppermute x0 -> x9, waiting for transfers between devices: none -> 38.4 us  [grp_swap(): return lax.ppermute(x, 'grp', [(i, i ^ bit) for i in range(n)])]
    psum x1 -> x0, waiting for transfers between devices: 32.2 us -> none  [local(): lax.psum(local_grad.astype(jnp.bfloat16), 'grp').astype(jnp.float32)]
    pallas_call x0 -> x5, Pallas kernels: none -> 29 us  [the longest x1 24.7 us: attend(): pl.pallas_call(functools.partial(attend_kernel, scale), out_shape=[jax.Sh...]
    all_to_all x3 -> x7, waiting for transfers between devices: 85 us -> 107 us  [seq_swap(): return lax.all_to_all(x, 'seq', split_axis=0, concat_axis=0, tiled=True)]
    convert_element_type x2 -> x0, local copies, waits for them, and re-layouts: 17.5 us -> none  [local(): dkeys.reshape(peers, per_peer, BLOCK_LEN * width).astype(jnp.bfloat16)]
    all_to_all x3 -> x7, starting transfers between devices: 16.7 us -> 32 us  [seq_swap(): return lax.all_to_all(x, 'seq', split_axis=0, concat_axis=0, tiled=True)]
  transfers between devices with their start and end apart: 6 -> 16, of which waited for: 5 -> 9; matrix products, arithmetic and copies ran while one was open for 10% -> 6% of each run, Pallas kernels for 0% -> 1%
where the time goes in v1:
time: 241 us; the launch traced here: 240 us
  waiting for transfers between devices  145 us (60%)
  starting transfers between devices  37.8 us (16%)
  Pallas kernels  29 us (12%)
  local copies, waits for them, and re-layouts  20.6 us (9%)
  other arithmetic  7.03 us (3%)
    all_to_all x7, waiting for transfers between devices, seq_swap(): return lax.all_to_all(x, 'seq', split_axis=0, concat_axis=0, tiled=True)  107 us
    ppermute x9, waiting for transfers between devices, grp_swap(): return lax.ppermute(x, 'grp', [(i, i ^ bit) for i in range(n)])  38.4 us
    all_to_all x7, starting transfers between devices, seq_swap(): return lax.all_to_all(x, 'seq', split_axis=0, concat_axis=0, tiled=True)  32 us
    pallas_call x1, Pallas kernels, attend(): pl.pallas_call(functools.partial(attend_kernel, scale), out_shape=[jax.Sh...  24.7 us
    unnamed x32, local copies, waits for them, and re-layouts  9.17 us
    ppermute x9, starting transfers between devices, grp_swap(): return lax.ppermute(x, 'grp', [(i, i ^ bit) for i in range(n)])  5.79 us
  transfers between devices with their start and end apart: 16, of which 9 were waited for; matrix products, arithmetic and copies ran while one was open for 6% of the time, Pallas kernels for 1%

profile of v1, /device:TPU:0, one launch (start us, length us, event | category | flops | bytes accessed | tf_op | source)
XLA Modules:
  0.0 240.2 jit_solution(3084677412601017225)
XLA Ops:
  0.6 0.5 broadcast.54
  1.1 1.3 reduce.11
  2.5 0.7 all_to_all.26
  3.1 7.3 %all-to-all-start.2 = ((s32[8,1,8]{2,1,0:T(1,128)}), s32[8,1,8]{2,1,0:T(1,128)S(1)}, u32[]{:S(2)}, u32[]{:S(2)}) async-start(s32[8,1,8]{2,1,0:T(1,128)} %bitcast.10), calls=%async_computation.2 | async-start | bytes 8192 | tf_op jit(solution)/shard_map/all_to_all | solution.py:37
  10.4 1.7 copy.50
  12.1 4.7 %all-to-all-done.2 = s32[8,1,8]{2,1,0:T(1,128)S(1)} async-done(((s32[8,1,8]{2,1,0:T(1,128)}), s32[8,1,8]{2,1,0:T(1,128)S(1)}, u32[]{:S(2)}, u32[]{:S(2)}) %all-to-all-start.2) | async-done | bytes 288 | tf_op jit(solution)/shard_map/all_to_all | solution.py:37
  16.8 0.7 fusion.2
  17.6 0.8 gather_fusion
  18.4 1.5 copy.52
  19.8 3.7 %all-to-all-start.3 = ((bf16[8,128,576]{1,2,0:T(8,128)(2,1)}), bf16[8,128,576]{1,2,0:T(8,128)(2,1)S(1)}, u32[]{:S(2)}, u32[]{:S(2)}) async-start(bf16[8,128,576]{1,2,0:T(8,128)(2,1)} %copy.52), calls=%async_computation.3 | async-start | bytes 2359296 | tf_op jit(solution)/shard_map/all_to_all | solution.py:37
  24.7 1.1 pad_maximum_fusion
  25.9 25.2 %all-to-all-done.3 = bf16[8,128,576]{1,2,0:T(8,128)(2,1)S(1)} async-done(((bf16[8,128,576]{1,2,0:T(8,128)(2,1)}), bf16[8,128,576]{1,2,0:T(8,128)(2,1)S(1)}, u32[]{:S(2)}, u32[]{:S(2)}) %all-to-all-start.3) | async-done | bytes 1179680 | tf_op jit(solution)/shard_map/all_to_all | solution.py:37
  51.1 1.0 copy-done.5
  52.1 3.6 %all-to-all-start = ((bf16[32,160,128]{2,1,0:T(8,128)(2,1)}), bf16[32,160,128]{2,1,0:T(8,128)(2,1)S(1)}, u32[]{:S(2)}, u32[]{:S(2)}) async-start(bf16[32,160,128]{2,1,0:T(8,128)(2,1)} %pad_maximum_fusion), calls=%async_computation | async-start | bytes 2621440 | tf_op jit(solution)/shard_map/all_to_all | solution.py:37
  55.7 1.7 copy.53
  57.4 1.6 collective-permute-start.1
  58.9 28.2 %all-to-all-done = bf16[32,160,128]{2,1,0:T(8,128)(2,1)S(1)} async-done(((bf16[32,160,128]{2,1,0:T(8,128)(2,1)}), bf16[32,160,128]{2,1,0:T(8,128)(2,1)S(1)}, u32[]{:S(2)}, u32[]{:S(2)}) %all-to-all-start) | async-done | bytes 1310752 | tf_op jit(solution)/shard_map/all_to_all | solution.py:37
  87.1 1.4 expand.1
  88.5 4.6 %all-to-all-start.1 = ((bf16[8,4,16,1024]{3,2,1,0:T(8,128)(2,1)}), bf16[8,4,16,1024]{3,2,1,0:T(8,128)(2,1)}, u32[]{:S(2)}, u32[]{:S(2)}) async-start(bf16[8,4,16,1024]{3,2,1,0:T(8,128)(2,1)} %expand.1), calls=%async_computation.1 | async-start | bytes 2097152 | tf_op jit(solution)/shard_map/all_to_all | solution.py:37
  93.1 0.5 collective-permute-start.2
  93.6 0.7 copy.49
  94.5 0.8 copy.54.bias
  95.3 1.9 collective-permute-done.refs_1_
  97.3 21.2 %all-to-all-done.1 = bf16[8,4,16,1024]{3,2,1,0:T(8,128)(2,1)} async-done(((bf16[8,4,16,1024]{3,2,1,0:T(8,128)(2,1)}), bf16[8,4,16,1024]{3,2,1,0:T(8,128)(2,1)}, u32[]{:S(2)}, u32[]{:S(2)}) %all-to-all-start.1) | async-done | bytes 1048608 | tf_op jit(solution)/shard_map/all_to_all | solution.py:37
  118.5 24.7 %attend.1 = (bf16[512,1024]{1,0:T(8,128)(2,1)}, bf16[512,64]{1,0:T(8,128)(2,1)}, bf16[64,16,576]{2,1,0:T(8,128)(2,1)}, bf16[64,16,576]{2,1,0:T(8,128)(2,1)}, bf1...) custom-call(bf16[512,1024]{1,0:T(8,128)(2,1)} %bitcast.5.qd, bf16[512,64]{1,0:T(8,128)(2,1)} %bitcast.46, ...), custom_call_target="tpu_custom_call" | custom-call | tf_op jit(solution)/shard_map/attend/pallas_call | solution.py:161
  143.2 3.6 %all-to-all-start.4 = ((bf16[8,4,16,1024]{3,2,1,0:T(8,128)(2,1)}), bf16[8,4,16,1024]{3,2,1,0:T(8,128)(2,1)S(1)}, u32[]{:S(2)}, u32[]{:S(2)}) async-start(bf16[8,4,16,1024]{3,2,1,0:T(8,128)(2,1)} %bitcast.43), calls=%async_computation.4 | async-start | bytes 2097152 | tf_op jit(solution)/shard_map/all_to_all | solution.py:37
  146.7 0.6 collective-permute-start.3
  147.3 2.1 add_convert_fusion.1
  149.5 1.6 collective-permute-start.5
  151.0 29.2 %collective-permute-done.5 = bf16[64,16,576]{2,1,0:T(8,128)(2,1)S(1)} collective-permute-done((bf16[64,16,576]{2,1,0:T(8,128)(2,1)S(1)}, bf16[64,16,576]{2,1,0:T(8,128)(2,1)S(1)}, u32[]{:S(2)}, u32[]{:S(2)}) %collective-permute-start.5) | collective-permute-done | bytes 1179680 | tf_op jit(solution)/shard_map/ppermute | solution.py:42
  180.2 1.6 add_convert_fusion
  181.8 2.4 %copy.58 = bf16[8,128,576]{1,2,0:T(8,128)(2,1)} copy(bf16[8,128,576]{2,1,0:T(8,128)(2,1)} %bitcast.34) | data formatting | bytes 2359296 | tf_op jit(solution)/shard_map/reshape | solution.py:266
  184.2 5.9 %all-to-all-start.6 = ((bf16[8,128,576]{1,2,0:T(8,128)(2,1)}), bf16[8,128,576]{1,2,0:T(8,128)(2,1)S(1)}, u32[]{:S(2)}, u32[]{:S(2)}) async-start(bf16[8,128,576]{1,2,0:T(8,128)(2,1)} %copy.58), calls=%async_computation.6 | async-start | bytes 2359296 | tf_op jit(solution)/shard_map/all_to_all | solution.py:37
  190.1 1.1 reduce.14
  191.2 27.2 %all-to-all-done.6 = bf16[8,128,576]{1,2,0:T(8,128)(2,1)S(1)} async-done(((bf16[8,128,576]{1,2,0:T(8,128)(2,1)}), bf16[8,128,576]{1,2,0:T(8,128)(2,1)S(1)}, u32[]{:S(2)}, u32[]{:S(2)}) %all-to-all-start.6) | async-done | bytes 1179680 | tf_op jit(solution)/shard_map/all_to_all | solution.py:37
  218.4 3.5 %all-to-all-start.5 = ((bf16[8,4,16,256]{3,2,1,0:T(8,128)(2,1)}), bf16[8,4,16,256]{3,2,1,0:T(8,128)(2,1)S(1)}, u32[]{:S(2)}, u32[]{:S(2)}) async-start(bf16[8,4,16,256]{3,2,1,0:T(8,128)(2,1)} %reduce.14), calls=%async_computation.5 | async-start | bytes 524288 | tf_op jit(solution)/shard_map/all_to_all | solution.py:37
  222.0 0.7 copy.59
  222.7 1.1 scatter.1.y0
  223.8 1.6 collective-permute-start.7
  225.3 0.7 copy.67
  226.0 7.2 %collective-permute-done.7.y2 = bf16[16,16,576]{2,1,0:T(8,128)(2,1)S(1)} collective-permute-done((bf16[16,16,576]{2,1,0:T(8,128)(2,1)S(1)}, bf16[16,16,576]{2,1,0:T(8,128)(2,1)S(1)}, u32[]{:S(2)}, u32[]{:S(2)}) %collective-permute-start.7) | collective-permute-done | bytes 294944 | tf_op jit(solution)/shard_map/ppermute | solution.py:42
  233.3 0.8 copy_bitcast_fusion
  234.0 0.7 copy-done
  234.8 0.7 copy-done.2
  235.6 1.0 copy-done.1
  236.5 1.0 copy-done.3
  237.5 0.7 assemble.1
  238.2 2.0 copy.60
  (49 shorter events, 1.7 us)
Async XLA Ops:
  3.1 13.7 %all-to-all-start.2 = ((s32[8,1,8]{2,1,0:T(1,128)}), s32[8,1,8]{2,1,0:T(1,128)S(1)}, u32[]{:S(2)}, u32[]{:S(2)}) async-start(s32[8,1,8]{2,1,0:T(1,128)} %bitcast.10), calls=%async_computation.2 | async-start | bytes 8192 | tf_op jit(solution)/shard_map/all_to_all | solution.py:37
  19.8 3.7 %copy-start.9 = (bf16[16,32,128]{2,1,0:T(8,128)(2,1)S(1)}, bf16[16,32,128]{2,1,0:T(8,128)(2,1)}, u32[]{:S(2)}) copy-start(bf16[16,32,128]{2,1,0:T(8,128)(2,1)} %param.8) | copy-start | bytes 393220
  19.8 3.8 %copy-start.10 = (bf16[16,32,128]{2,1,0:T(8,128)(2,1)S(1)}, bf16[16,32,128]{2,1,0:T(8,128)(2,1)}, u32[]{:S(2)}) copy-start(bf16[16,32,128]{2,1,0:T(8,128)(2,1)} %param.13) | copy-start | bytes 393220
  19.8 3.9 %copy-start.7 = (bf16[32,8192]{1,0:T(8,128)(2,1)S(1)}, bf16[32,8192]{1,0:T(8,128)(2,1)}, u32[]{:S(2)}) copy-start(bf16[32,8192]{1,0:T(8,128)(2,1)} %param.11) | copy-start | bytes 1572868
  19.8 31.2 %all-to-all-start.3 = ((bf16[8,128,576]{1,2,0:T(8,128)(2,1)}), bf16[8,128,576]{1,2,0:T(8,128)(2,1)S(1)}, u32[]{:S(2)}, u32[]{:S(2)}) async-start(bf16[8,128,576]{1,2,0:T(8,128)(2,1)} %copy.52), calls=%async_computation.3 | async-start | bytes 2359296 | tf_op jit(solution)/shard_map/all_to_all | solution.py:37
  23.5 1.0 copy-start.8
  51.1 1.0 copy-start.5
  52.1 35.0 %all-to-all-start = ((bf16[32,160,128]{2,1,0:T(8,128)(2,1)}), bf16[32,160,128]{2,1,0:T(8,128)(2,1)S(1)}, u32[]{:S(2)}, u32[]{:S(2)}) async-start(bf16[32,160,128]{2,1,0:T(8,128)(2,1)} %pad_maximum_fusion), calls=%async_computation | async-start | bytes 2621440 | tf_op jit(solution)/shard_map/all_to_all | solution.py:37
  57.4 35.7 %copy-start.4 = (bf16[8,128,576]{2,1,0:T(8,128)(2,1)}, bf16[8,128,576]{2,1,0:T(8,128)(2,1)S(1)}, u32[]{:S(2)}) copy-start(bf16[8,128,576]{2,1,0:T(8,128)(2,1)S(1)} %copy.53) | copy-start | bytes 3538948
  57.4 35.8 %collective-permute-start.1 = (bf16[64,16,576]{2,1,0:T(8,128)(2,1)S(1)}, bf16[64,16,576]{2,1,0:T(8,128)(2,1)}, u32[]{:S(2)}, u32[]{:S(2)}) collective-permute-start(bf16[64,16,576]{2,1,0:T(8,128)(2,1)S(1)} %bitcast.37), channel_id=1, source_target_pairs={{0,2},{1,3},{2,0},{3,1},{4,6},{5,7},{6,4},{7,5},{8,10},{9,11},{10,... | collective-permute-start | bytes 3538952 | tf_op jit(solution)/shard_map/ppermute | solution.py:42
  88.5 5.2 %copy-start.11 = (bf16[16,32,64]{2,1,0:T(8,128)(2,1)S(1)}, bf16[16,32,64]{2,1,0:T(8,128)(2,1)}, u32[]{:S(2)}) copy-start(bf16[16,32,64]{2,1,0:T(8,128)(2,1)} %param.9) | copy-start | bytes 196612
  88.5 5.9 %copy-start.13 = (s32[16,32]{1,0:T(8,128)S(1)}, s32[16,32]{1,0:T(8,128)}, u32[]{:S(2)}) copy-start(s32[16,32]{1,0:T(8,128)} %param.14) | copy-start | bytes 6148
  88.5 30.0 %all-to-all-start.1 = ((bf16[8,4,16,1024]{3,2,1,0:T(8,128)(2,1)}), bf16[8,4,16,1024]{3,2,1,0:T(8,128)(2,1)}, u32[]{:S(2)}, u32[]{:S(2)}) async-start(bf16[8,4,16,1024]{3,2,1,0:T(8,128)(2,1)} %expand.1), calls=%async_computation.1 | async-start | bytes 2097152 | tf_op jit(solution)/shard_map/all_to_all | solution.py:37
  93.1 4.2 %collective-permute-start = (bf16[64,16,576]{2,1,0:T(8,128)(2,1)S(1)}, bf16[64,16,576]{2,1,0:T(8,128)(2,1)}, u32[]{:S(2)}, u32[]{:S(2)}) collective-permute-start(bf16[64,16,576]{2,1,0:T(8,128)(2,1)S(1)} %bitcast.38), channel_id=1, source_target_pairs={{0,1},{1,0},{2,3},{3,2},{4,5},{5,4},{6,7},{7,6},{8,9},{9,8},{10,11... | collective-permute-start | bytes 3538952 | tf_op jit(solution)/shard_map/ppermute | solution.py:42
  93.1 25.3 %collective-permute-start.2 = (bf16[64,16,576]{2,1,0:T(8,128)(2,1)}, bf16[64,16,576]{2,1,0:T(8,128)(2,1)}, u32[]{:S(2)}, u32[]{:S(2)}) collective-permute-start(bf16[64,16,576]{2,1,0:T(8,128)(2,1)} %collective-permute-done.1.refs_2_), channel_id=1, source_target_pairs={{0,1},{1,0},{2,3},{3,2},{4,5},{5,4},{6,7},{7,6},{8,9},{9,8},{10,11... | collective-permute-start | bytes 3538952 | tf_op jit(solution)/shard_map/ppermute | solution.py:42
  143.2 4.1 %collective-permute-start.4 = (bf16[64,16,576]{2,1,0:T(8,128)(2,1)}, bf16[64,16,576]{2,1,0:T(8,128)(2,1)}, u32[]{:S(2)}, u32[]{:S(2)}) collective-permute-start(bf16[64,16,576]{2,1,0:T(8,128)(2,1)} %get-tuple-element.15), channel_id=1, source_target_pairs={{0,1},{1,0},{2,3},{3,2},{4,5},{5,4},{6,7},{7,6},{8,9},{9,8},{10,11... | collective-permute-start | bytes 3538952 | tf_op jit(solution)/shard_map/ppermute | solution.py:42
  143.2 41.0 %all-to-all-start.4 = ((bf16[8,4,16,1024]{3,2,1,0:T(8,128)(2,1)}), bf16[8,4,16,1024]{3,2,1,0:T(8,128)(2,1)S(1)}, u32[]{:S(2)}, u32[]{:S(2)}) async-start(bf16[8,4,16,1024]{3,2,1,0:T(8,128)(2,1)} %bitcast.43), calls=%async_computation.4 | async-start | bytes 2097152 | tf_op jit(solution)/shard_map/all_to_all | solution.py:37
  146.7 4.3 %collective-permute-start.3 = (bf16[64,16,576]{2,1,0:T(8,128)(2,1)}, bf16[64,16,576]{2,1,0:T(8,128)(2,1)S(1)}, u32[]{:S(2)}, u32[]{:S(2)}) collective-permute-start(bf16[64,16,576]{2,1,0:T(8,128)(2,1)} %get-tuple-element.13), channel_id=1, source_target_pairs={{0,1},{1,0},{2,3},{3,2},{4,5},{5,4},{6,7},{7,6},{8,9},{9,8},{10,11... | collective-permute-start | bytes 3538952 | tf_op jit(solution)/shard_map/ppermute | solution.py:42
  147.3 32.9 %copy-start.6 = (bf16[64,16,576]{2,1,0:T(8,128)(2,1)S(1)}, bf16[64,16,576]{2,1,0:T(8,128)(2,1)}, u32[]{:S(2)}) copy-start(bf16[64,16,576]{2,1,0:T(8,128)(2,1)} %get-tuple-element.12) | copy-start | bytes 3538948
  149.5 30.8 %collective-permute-start.5 = (bf16[64,16,576]{2,1,0:T(8,128)(2,1)S(1)}, bf16[64,16,576]{2,1,0:T(8,128)(2,1)S(1)}, u32[]{:S(2)}, u32[]{:S(2)}) collective-permute-start(bf16[64,16,576]{2,1,0:T(8,128)(2,1)S(1)} %add_convert_fusion.1), channel_id=1, source_target_pairs={{0,2},{1,3},{2,0},{3,1},{4,6},{5,7},{6,4},{7,5},{8,10},{9,11},{10,... | collective-permute-start | bytes 3538952 | tf_op jit(solution)/shard_map/ppermute | solution.py:42
  184.2 34.2 %all-to-all-start.6 = ((bf16[8,128,576]{1,2,0:T(8,128)(2,1)}), bf16[8,128,576]{1,2,0:T(8,128)(2,1)S(1)}, u32[]{:S(2)}, u32[]{:S(2)}) async-start(bf16[8,128,576]{1,2,0:T(8,128)(2,1)} %copy.58), calls=%async_computation.6 | async-start | bytes 2359296 | tf_op jit(solution)/shard_map/all_to_all | solution.py:37
  218.4 14.8 %all-to-all-start.5 = ((bf16[8,4,16,256]{3,2,1,0:T(8,128)(2,1)}), bf16[8,4,16,256]{3,2,1,0:T(8,128)(2,1)S(1)}, u32[]{:S(2)}, u32[]{:S(2)}) async-start(bf16[8,4,16,256]{3,2,1,0:T(8,128)(2,1)} %reduce.14), calls=%async_computation.5 | async-start | bytes 524288 | tf_op jit(solution)/shard_map/all_to_all | solution.py:37
  222.7 2.6 %copy-start.12 = (bf16[512,64]{1,0:T(8,128)(2,1)S(1)}, bf16[512,64]{1,0:T(8,128)(2,1)}, u32[]{:S(2)}) copy-start(bf16[512,64]{1,0:T(8,128)(2,1)} %get-tuple-element.11) | copy-start | bytes 196612
  223.8 9.4 %collective-permute-start.7 = (bf16[16,16,576]{2,1,0:T(8,128)(2,1)S(1)}, bf16[16,16,576]{2,1,0:T(8,128)(2,1)S(1)}, u32[]{:S(2)}, u32[]{:S(2)}) collective-permute-start(bf16[16,16,576]{2,1,0:T(8,128)(2,1)S(1)} %scatter.1.y0), channel_id=1, source_target_pairs={{0,2},{1,3},{2,0},{3,1},{4,6},{5,7},{6,4},{7,5},{8,10},{9,11},{10,... | collective-permute-start | bytes 884744 | tf_op jit(solution)/shard_map/ppermute | solution.py:42
  226.0 8.0 %collective-permute-start.6 = (bf16[16,16,576]{2,1,0:T(8,128)(2,1)S(1)}, bf16[16,16,576]{2,1,0:T(8,128)(2,1)S(1)}, u32[]{:S(2)}, u32[]{:S(2)}) collective-permute-start(bf16[16,16,576]{2,1,0:T(8,128)(2,1)S(1)} %scatter.1.y0), channel_id=1, source_target_pairs={{0,1},{1,0},{2,3},{3,2},{4,5},{5,4},{6,7},{7,6},{8,9},{9,8},{10,11... | collective-permute-start | bytes 884744 | tf_op jit(solution)/shard_map/ppermute | solution.py:42
  233.2 1.6 collective-permute-start.8
  234.0 0.7 copy-start
  234.8 0.7 copy-start.2
  235.6 1.0 copy-start.1
  236.5 1.0 copy-start.3

commit v2 on v0

--- a/solution.py
+++ b/solution.py
@@ -1,14 +1,490 @@
+import functools
 import math
 
 import jax
 import jax.numpy as jnp
 from jax import lax
+from jax.experimental import pallas as pl
+from jax.experimental.pallas import tpu as pltpu
 from jax.sharding import PartitionSpec as P
 
 BLOCK_LEN = 64
+LANES = 128
+HIDDEN = -1e30
+SPAN = 4
+VMEM = pl.BlockSpec(memory_space=pltpu.VMEM)
+SMEM = pl.BlockSpec(memory_space=pltpu.SMEM)
+ANY = pl.BlockSpec(memory_space=pl.ANY)
+F32 = jnp.float32
+BF16 = jnp.bfloat16
+
+
+def call(kernel, name, args, specs, outs, scratch=(), mib=32):
+    return pl.pallas_call(
+        kernel,
+        out_shape=[jax.ShapeDtypeStruct(s, d) for s, d in outs],
+        in_specs=specs,
+        out_specs=[VMEM] * len(outs),
+        scratch_shapes=list(scratch),
+        compiler_params=pltpu.CompilerParams(vmem_limit_bytes=mib * 2**20),
+        name=name,
+    )(*args)
+
+
+def nt(a, b):
+    return lax.dot_general(a, b, (((1,), (1,)), ((), ())), preferred_element_type=F32)
+
+
+def nn(a, b):
+    return lax.dot_general(a, b, (((1,), (0,)), ((), ())), preferred_element_type=F32)
+
+
+def swap(x, axis, bit):
+    n = lax.axis_size(axis)
+    return lax.ppermute(x, axis, [(i, i ^ bit) for i in range(n)])
+
+
+def exchange(pieces):
+    return [pieces[0]] + [swap(p, "seq", k) for k, p in enumerate(pieces) if k > 0]
+
+
+def gather_kernel(count, ids, *refs):
+    rows, cache, outs = refs[:count], refs[count], refs[count + 1 :]
+    me, grp = ids[0], ids[1]
+    depth, lanes = outs[0].shape
+    per_peer = lanes // BLOCK_LEN
+    part = pl.ds(pl.multiple_of(grp * depth, 16), depth)
+
+    def block(k, j):
+        b = rows[k][0, me * per_peer + j]
+        tile = cache[part, pl.ds(pl.multiple_of((b >> 1) * LANES, LANES), LANES)]
+        return jnp.where((b & 1) == 1, tile[:, BLOCK_LEN:], tile[:, :BLOCK_LEN])
+
+    for k in range(count):
+        for j in range(0, per_peer, 2):
+            both = jnp.concatenate([block(k, j), block(k, j + 1)], axis=1)
+            outs[k][:, j * BLOCK_LEN : (j + 2) * BLOCK_LEN] = both
+
+
+def scatter_kernel(count, ids, *refs):
+    rows, got, out, acc = refs[:count], refs[count : 2 * count], refs[2 * count], refs[2 * count + 1]
+    me = ids[0]
+    depth, lanes = got[0].shape
+    per_peer = lanes // BLOCK_LEN
+    acc[...] = jnp.zeros_like(acc)
+    blank = jnp.zeros((depth, BLOCK_LEN), F32)
+    for k in range(count):
+        for j in range(per_peer):
+            b = rows[k][0, me * per_peer + j]
+            at = pl.ds(pl.multiple_of((b >> 1) * LANES, LANES), LANES)
+            g = got[k][:, j * BLOCK_LEN : (j + 1) * BLOCK_LEN].astype(F32)
+            low = jnp.concatenate([g, blank], axis=1)
+            high = jnp.concatenate([blank, g], axis=1)
+            acc[:, at] = acc[:, at] + jnp.where((b & 1) == 1, high, low)
+    out[...] = acc[...].astype(BF16)
+
+
+def assemble_kernel(ids, *refs):
+    parts, out = refs[:-1], refs[-1]
+    depth = parts[0].shape[0]
+    for k, y in enumerate(parts):
+        out[pl.ds(pl.multiple_of((ids[1] ^ k) * depth, 16), depth), :] = y[...].astype(F32)
+
+
+def pack_kernel(span, ids, weight, vec, *refs):
+    outs = refs[-lax.axis_size("seq") :]
+    share = weight.shape[0] // span
+    rows = weight.shape[1]
+    for k, out in enumerate(outs):
+        at = pl.ds(((ids[0] ^ k) & (span - 1)) * share, share)
+        out[:, :rows] = weight[at]
+        if k < span:
+            out[:, rows:] = vec[at]
+
+
+def expand_k_kernel(span, queries, ids, *refs):
+    peers = lax.axis_size("seq")
+    got, outs, whole = refs[:peers], refs[peers : peers + span], refs[peers + span]
+    share, nope, latent = whole.shape
+    n_rows = nope // peers
+    tiles = latent // LANES
+    for h in range(share):
+        for k in range(peers):
+            at = pl.ds(pl.multiple_of((ids[0] ^ k) * n_rows, 16), n_rows)
+            for t in range(tiles):
+                whole[h, at, t * LANES : (t + 1) * LANES] = got[k][h, t * n_rows : (t + 1) * n_rows]
+        q = jnp.concatenate([got[k][h, n_rows * tiles :] for k in range(span)], axis=0)
+        res = nn(q, whole[h]).astype(BF16)
+        for k in range(span):
+            outs[k][h] = res[k * queries : (k + 1) * queries]
+
+
+def expand_v_kernel(span, queries, ids, *refs):
+    peers = lax.axis_size("seq")
+    got, outs, whole = refs[:peers], refs[peers : peers + span], refs[peers + span]
+    share, latent, value = whole.shape
+    l_rows = latent // peers
+    for h in range(share):
+        for k in range(peers):
+            at = pl.ds(pl.multiple_of((ids[0] ^ k) * l_rows, 16), l_rows)
+            whole[h, at, :] = got[k][h, :l_rows]
+        d = jnp.concatenate([got[k][h, l_rows:] for k in range(span)], axis=0)
+        res = nt(d, whole[h]).astype(BF16)
+        for k in range(span):
+            outs[k][h] = res[k * queries : (k + 1) * queries]
+
+
+def reduce_kernel(span, queries, wk, wv, *refs):
+    o, d, outs = refs[:span], refs[span : 2 * span], refs[2 * span :]
+    value = wv.shape[2]
+    for h in range(wk.shape[0]):
+        attn = nn(jnp.concatenate([o[k][h] for k in range(span)], axis=0), wv[h]).astype(BF16)
+        dqn = nt(jnp.concatenate([d[k][h] for k in range(span)], axis=0), wk[h]).astype(BF16)
+        for k in range(span):
+            outs[k][h, :, :value] = attn[k * queries : (k + 1) * queries]
+            outs[k][h, :, value:] = dqn[k * queries : (k + 1) * queries]
+
+
+def place_kernel(span, ids, *refs):
+    got, attn, dqn = refs[:span], refs[span], refs[span + 1]
+    value = attn.shape[2]
+    share = got[0].shape[0]
+    for k in range(span):
+        at = pl.ds(((ids[0] ^ k) & (span - 1)) * share, share)
+        attn[at] = got[k][:, :, :value]
+        dqn[at] = got[k][:, :, value:]
+
+
+def rope_at(ids, k, span, share):
+    return pl.ds(((ids[0] ^ k) & (span - 1)) * share, share)
+
+
+def forward_kernel(scale, span, per_peer, ids, sel, rope, *refs):
+    q_lat, refs = refs[:span], refs[span:]
+    keys, refs = (refs[:4], refs[4:8]), refs[8:]
+    kts, pbs, refs = refs[:2], refs[2:4], refs[4:]
+    o_out, o_full, qx, sc = refs[:span], refs[span], refs[span + 1], refs[span + 2]
+    share, queries, latent = q_lat[0].shape
+    rope_dim = rope.shape[2]
+    width = latent + rope_dim
+    span_rows = share * queries
+    rows = span * span_rows
+    slots = qx.shape[1] - width
+    held, depth, lanes = keys[0][0].shape
+    half = held * lanes
+
+    picks = sel[...] ^ (ids[0] * per_peer)
+    slot = lax.broadcasted_iota(jnp.int32, (queries, slots), 1)
+    chosen = picks[:, 0:1] == slot
+    for j in range(1, picks.shape[1]):
+        chosen = chosen | (picks[:, j : j + 1] == slot)
+    bias = jnp.where(chosen, 0.0, HIDDEN).astype(BF16)
+    bias = jnp.broadcast_to(bias[None], (share, queries, slots)).reshape(span_rows, slots)
+    for k in range(span):
+        at = slice(k * span_rows, (k + 1) * span_rows)
+        qx[at, :latent] = q_lat[k][...].reshape(span_rows, latent)
+        tail = rope[rope_at(ids, k, span, share)].reshape(span_rows, rope_dim)
+        qx[at, latent:] = jnp.concatenate([tail, bias], axis=1)
+    for c in range(2):
+        for k in range(4):
+            at = pl.ds(pl.multiple_of((ids[1] ^ k) * depth, 16), depth)
+            for i in range(held):
+                kts[c][at, i * lanes : (i + 1) * lanes] = keys[c][k][i]
+        place = lax.broadcasted_iota(jnp.int32, (slots, half), 0)
+        token = lax.broadcasted_iota(jnp.int32, (slots, half), 1) + c * half
+        kts[c][width:, :] = jnp.where(token // BLOCK_LEN == place, 1.0, 0.0).astype(BF16)
+
+    scale2 = scale * math.log2(math.e)
+    step = 512
+    chunks = [(c, i) for c in range(2) for i in range(0, half, step)]
+    top = jnp.full((rows, 1), -jnp.inf, F32)
+    for n, (c, i) in enumerate(chunks):
+        s = nn(qx[...], kts[c][:, i : i + step]) * scale2
+        sc[:, n * step : (n + 1) * step] = s
+        top = jnp.maximum(top, jnp.max(s, axis=1, keepdims=True))
+    total = jnp.zeros((rows, 1), F32)
+    for n in range(len(chunks)):
+        e = jnp.exp2(sc[:, n * step : (n + 1) * step] - top)
+        sc[:, n * step : (n + 1) * step] = e
+        total = total + jnp.sum(e, axis=1, keepdims=True)
+    inv = 1.0 / total
+    for n, (c, i) in enumerate(chunks):
+        pb = (sc[:, n * step : (n + 1) * step] * inv).astype(BF16)
+        pbs[c][:, i : i + step] = pb
+        part = nt(pb, kts[c][:latent, i : i + step])
+        if n == 0:
+            o_full[...] = part
+        else:
+            o_full[...] += part
+    for k in range(span):
+        o = o_full[k * span_rows : (k + 1) * span_rows].astype(BF16)
+        o_out[k][...] = o.reshape(share, queries, latent)
+
+
+def backward_kernel(scale, span, first, ids, rope, o_full, kt, pb, *refs):
+    q_lat, refs = refs[:span], refs[span:]
+    d_olat, refs = refs[:span], refs[span:]
+    if not first:
+        before, refs = refs[0], refs[1:]
+    send, keep, refs = refs[0], refs[1], refs[2:]
+    if first:
+        dq, refs = refs[0], refs[1:]
+    else:
+        d_lat, d_rope, refs = refs[:span], refs[span], refs[span + 1 :]
+    qf, do, flip, cat = refs[:4]
+    if not first:
+        dq = refs[4]
+    share, queries, latent = q_lat[0].shape
+    rope_dim = rope.shape[2]
+    width = latent + rope_dim
+    span_rows = share * queries
+    rows = span * span_rows
+    depth = width // 4
+    for k in range(span):
+        at = slice(k * span_rows, (k + 1) * span_rows)
+        qf[at, :latent] = q_lat[k][...].reshape(span_rows, latent)
+        qf[at, latent:] = rope[rope_at(ids, k, span, share)].reshape(span_rows, rope_dim)
+        do[at, :] = d_olat[k][...].reshape(span_rows, latent)
+    flip[:, :rows] = qf[...].T
+    flip[:latent, rows:] = do[...].T
+    flip[latent:, rows:] = jnp.zeros((rope_dim, rows), BF16)
+    for k in range(4):
+        at = pl.ds(pl.multiple_of((ids[1] ^ k) * depth, 16), depth)
+        cat[k * depth : (k + 1) * depth] = flip[at, :]
+    delta = jnp.sum(o_full[...] * do[...].astype(F32), axis=1, keepdims=True)
+    step = 512
+    for n, i in enumerate(range(0, pb.shape[1], step)):
+        at = slice(i, i + step)
+        p = pb[:, at]
+        dp = nn(do[...], kt[:latent, at])
+        ds = (p.astype(F32) * (dp - delta) * scale).astype(BF16)
+        part = nt(ds, kt[:width, at])
+        if n > 0:
+            dq[...] += part
+        elif first:
+            dq[...] = part
+        else:
+            dq[...] = before[...] + part
+        dk = nn(cat[...], jnp.concatenate([ds, p], axis=0)).astype(BF16)
+        for k, ref in enumerate((keep, send, keep, send)):
+            ref[k // 2, :, at] = dk[k * depth : (k + 1) * depth]
+    if not first:
+        for k in range(span):
+            at = slice(k * span_rows, (k + 1) * span_rows)
+            d_lat[k][...] = dq[at, :latent].astype(BF16).reshape(share, queries, latent)
+            d_rope[rope_at(ids, k, span, share)] = (
+                dq[at, latent:].astype(BF16).reshape(share, queries, rope_dim)
+            )
+
+
+def pair_kernel(keep, got, a0, *a2):
+    total = keep[...].astype(F32) + got[...].astype(F32)
+    a0[...] = total[0].astype(BF16)
+    lanes = a2[0].shape[1]
+    for i, a in enumerate(a2):
+        a[...] = total[1, :, i * lanes : (i + 1) * lanes].astype(BF16)
+
+
+def owner_kernel(a0, got, *outs):
+    total = (a0[...].astype(F32) + got[...].astype(F32)).astype(BF16)
+    lanes = outs[0].shape[1]
+    for i, out in enumerate(outs):
+        out[...] = total[:, i * lanes : (i + 1) * lanes]
 
 
 def local(q_nope, q_rope, cache, w_uk, w_uv, d_out, sel, slot_blocks):
+    peers = lax.axis_size("seq")
+    groups = lax.axis_size("grp")
+    queries, heads, nope = q_nope.shape
+    rope = q_rope.shape[2]
+    width = cache.shape[1]
+    latent = width - rope
+    value = d_out.shape[2]
+    slots = slot_blocks.shape[1]
+    per_peer = slots // peers
+    if not (peers == 8 and groups == 4 and heads % SPAN == 0 and per_peer % 2 == 0):
+        return local_general(q_nope, q_rope, cache, w_uk, w_uv, d_out, sel, slot_blocks)
+    ids = jnp.stack([lax.axis_index("seq"), lax.axis_index("grp")]).astype(jnp.int32)
+    tokens = cache.shape[0]
+    depth = width // groups
+    lanes = per_peer * BLOCK_LEN
+    held = peers // 2
+    half = held * lanes
+    share = heads // SPAN
+    rows = heads * queries
+    scale = 1.0 / math.sqrt(nope + rope)
+
+    asked = exchange([slot_blocks] * peers)
+    mine = call(
+        functools.partial(gather_kernel, peers),
+        "gather",
+        (ids, *asked, cache.T),
+        [SMEM] * (1 + peers) + [VMEM],
+        [((depth, lanes), BF16)] * peers,
+    )
+    arrived = exchange(mine)
+    keys = []
+    for c in range(2):
+        k0 = jnp.stack(arrived[c * held : (c + 1) * held])
+        k2 = swap(k0, "grp", 2)
+        k1 = swap(k0, "grp", 1)
+        k3 = swap(k2, "grp", 1)
+        keys.append((k0, k1, k2, k3))
+
+    n_rows = w_uk.shape[1] // latent
+    l_rows = w_uv.shape[1] // value
+    tiles = latent // LANES
+    uk = w_uk.reshape(heads, n_rows, tiles, LANES).transpose(0, 2, 1, 3)
+    uk = uk.reshape(heads, n_rows * tiles, LANES)
+    uv = w_uv.reshape(heads, l_rows, value)
+
+    def pieces(w_rows):
+        return [
+            ((share, w_rows + (queries if k < SPAN else 0), LANES), BF16) for k in range(peers)
+        ]
+
+    lat_shape = ((share, queries, latent), BF16)
+    packed = call(
+        functools.partial(pack_kernel, SPAN),
+        "pack_k",
+        (ids, uk, q_nope.transpose(1, 0, 2)),
+        [SMEM, VMEM, VMEM],
+        pieces(n_rows * tiles),
+    )
+    *q_lat, wk = call(
+        functools.partial(expand_k_kernel, SPAN, queries),
+        "expand_k",
+        (ids, *exchange(packed)),
+        [SMEM] + [VMEM] * peers,
+        [lat_shape] * SPAN + [((share, nope, latent), BF16)],
+    )
+    packed = call(
+        functools.partial(pack_kernel, SPAN),
+        "pack_v",
+        (ids, uv, d_out.transpose(1, 0, 2), wk),
+        [SMEM, VMEM, VMEM, ANY],
+        pieces(l_rows),
+    )
+    q_lat = exchange(q_lat)
+    *d_olat, wv = call(
+        functools.partial(expand_v_kernel, SPAN, queries),
+        "expand_v",
+        (ids, *exchange(packed)),
+        [SMEM] + [VMEM] * peers,
+        [lat_shape] * SPAN + [((share, latent, value), BF16)],
+    )
+    d_olat = exchange(d_olat)
+
+    rope_rows = q_rope.transpose(1, 0, 2)
+    kt0, kt1, pb0, pb1, *o_lat, o_full = call(
+        functools.partial(forward_kernel, scale, SPAN, per_peer),
+        "forward",
+        (ids, sel, rope_rows, *q_lat, *keys[0], *keys[1]),
+        [SMEM] + [VMEM] * (2 + SPAN + 8),
+        [((width + slots, half), BF16)] * 2
+        + [((rows, half), BF16)] * 2
+        + [lat_shape] * SPAN
+        + [((rows, latent), F32)],
+        [pltpu.VMEM((rows, width + slots), BF16), pltpu.VMEM((rows, 2 * half), F32)],
+        48,
+    )
+    o_lat = exchange(o_lat)
+
+    def backward(kt, pb, before):
+        first = before is None
+        outs = [((2, depth, half), BF16)] * 2
+        scratch = [
+            pltpu.VMEM((rows, width), BF16),
+            pltpu.VMEM((rows, latent), BF16),
+            pltpu.VMEM((width, 2 * rows), BF16),
+            pltpu.VMEM((width, 2 * rows), BF16),
+        ]
+        if first:
+            outs = outs + [((rows, width), F32)]
+        else:
+            outs = outs + [lat_shape] * SPAN + [((heads, queries, rope), BF16)]
+            scratch = scratch + [pltpu.VMEM((rows, width), F32)]
+        args = (ids, rope_rows, o_full, kt, pb, *q_lat, *d_olat) + (() if first else (before,))
+        return call(
+            functools.partial(backward_kernel, scale, SPAN, first),
+            "backward_far" if first else "backward_near",
+            args,
+            [SMEM] + [VMEM] * (len(args) - 1),
+            outs,
+            scratch,
+            40,
+        )
+
+    def give(send, keep, splits):
+        got = swap(send, "grp", 1)
+        a0, *a2 = call(
+            pair_kernel,
+            "pair",
+            (keep, got),
+            [VMEM, VMEM],
+            [((depth, half), BF16)] + [((depth, half // splits), BF16)] * splits,
+        )
+        out = []
+        for i, a in enumerate(a2):
+            size = half // splits
+            out += call(
+                owner_kernel,
+                "owner",
+                (a0[:, i * size : (i + 1) * size], swap(a, "grp", 2)),
+                [VMEM, VMEM],
+                [((depth, lanes), BF16)] * (size // lanes),
+            )
+        return out
+
+    send, keep, dq = backward(kt1, pb1, None)
+    far = give(send, keep, 2)
+    send, keep, *rest = backward(kt0, pb0, dq)
+    near = give(send, keep, 1)
+    d_lat, d_rope = exchange(rest[:SPAN]), rest[SPAN]
+    got = exchange(near + far)
+
+    res = call(
+        functools.partial(reduce_kernel, SPAN, queries),
+        "reduce",
+        (wk, wv, *o_lat, *d_lat),
+        [VMEM] * (2 + 2 * SPAN),
+        [((share, queries, value + nope), BF16)] * SPAN,
+    )
+    attn_out, d_q_nope = call(
+        functools.partial(place_kernel, SPAN),
+        "place",
+        (ids, *exchange(res)),
+        [SMEM] + [VMEM] * SPAN,
+        [((heads, queries, value), BF16), ((heads, queries, nope), BF16)],
+    )
+
+    (y0,) = call(
+        functools.partial(scatter_kernel, peers),
+        "scatter",
+        (ids, *asked, *got),
+        [SMEM] * (1 + peers) + [VMEM] * peers,
+        [((depth, tokens), BF16)],
+        [pltpu.VMEM((depth, tokens), F32)],
+    )
+    y2 = swap(y0, "grp", 2)
+    y1 = swap(y0, "grp", 1)
+    y3 = swap(y2, "grp", 1)
+    (d_cache,) = call(
+        assemble_kernel,
+        "assemble",
+        (ids, y0, y1, y2, y3),
+        [SMEM] + [VMEM] * 4,
+        [((width, tokens), F32)],
+    )
+    return (
+        attn_out.transpose(1, 0, 2),
+        d_q_nope.transpose(1, 0, 2),
+        d_rope.transpose(1, 0, 2),
+        d_cache.T,
+    )
+
+
+def local_general(q_nope, q_rope, cache, w_uk, w_uv, d_out, sel, slot_blocks):
     peers = lax.axis_size("seq")
     queries, heads, nope = q_nope.shape
     rope = q_rope.shape[2]

time: 482 us -> 236 us (0.49)
  waiting for transfers between devices: 328 us -> 102 us
  matrix products: 77.5 us -> 0 us
  starting transfers between devices: 17.1 us -> 89.3 us
  Pallas kernels: 0 us -> 35.2 us
  local copies, waits for them, and re-layouts: 42.2 us -> 8.5 us
  between operations: 13.9 us -> 0.98 us
    all_gather x2 -> x0, waiting for transfers between devices: 210 us -> none  [the longest x1 141 us: local(): lax.all_gather(w_uk, 'seq', axis=1, tiled=True)]
    ppermute x0 -> x64, waiting for transfers between devices: none -> 102 us  [swap(): return lax.ppermute(x, axis, [(i, i ^ bit) for i in range(n)])]
    ppermute x0 -> x64, starting transfers between devices: none -> 89.3 us  [swap(): return lax.ppermute(x, axis, [(i, i ^ bit) for i in range(n)])]
    all_to_all x3 -> x0, waiting for transfers between devices: 85 us -> none  [the longest x1 80.2 us: local(): lax.all_to_all(dkeys.reshape(peers, per_peer, BLOCK_LEN * width).astype(j...]
    dot_general x10 -> x0, matrix products: 66.8 us -> none  [the longest x1 18.7 us: local(): jnp.einsum('qht,qhc->tc', dscore, qfull, preferred_element_type=jnp.float32)]
    pallas_call x0 -> x17, Pallas kernels: none -> 35.2 us  [call(): pl.pallas_call(kernel, out_shape=[jax.ShapeDtypeStruct(s, d) for s, d in...]
    psum x1 -> x0, waiting for transfers between devices: 32.2 us -> none  [local(): lax.psum(local_grad.astype(jnp.bfloat16), 'grp').astype(jnp.float32)]
    convert_element_type x2 -> x0, local copies, waits for them, and re-layouts: 17.5 us -> none  [local(): dkeys.reshape(peers, per_peer, BLOCK_LEN * width).astype(jnp.bfloat16)]
  transfers between devices with their start and end apart: 6 -> 64, of which waited for: 5 -> 31; matrix products, arithmetic and copies ran while one was open for 10% -> 1% of each run, Pallas kernels for 0% -> 8%
where the time goes in v2:
time: 236 us
  waiting for transfers between devices  102 us (43%)
  starting transfers between devices  89.3 us (38%)
  Pallas kernels  35.2 us (15%)
  local copies, waits for them, and re-layouts  8.5 us (4%)
    ppermute x64, waiting for transfers between devices, swap(): return lax.ppermute(x, axis, [(i, i ^ bit) for i in range(n)])  102 us
    ppermute x64, starting transfers between devices, swap(): return lax.ppermute(x, axis, [(i, i ^ bit) for i in range(n)])  89.3 us
    pallas_call x17, Pallas kernels, call(): pl.pallas_call(kernel, out_shape=[jax.ShapeDtypeStruct(s, d) for s, d in...  35.2 us
    unnamed x31, local copies, waits for them, and re-layouts  6.93 us
  transfers between devices with their start and end apart: 64, of which 31 were waited for; matrix products, arithmetic and copies ran while one was open for 1% of the time, Pallas kernels for 8%

profile of v2, /device:TPU:0, one launch (start us, length us, event | category | flops | bytes accessed | tf_op | source)
XLA Modules:
  0.0 235.9 jit_solution(14365427101051734964)
XLA Ops:
  3.0 4.1 %collective-permute-start.3 = (bf16[8,64,128]{2,1,0:T(8,128)(2,1)S(1)}, bf16[8,64,128]{2,1,0:T(8,128)(2,1)S(1)}, u32[]{:S(2)}, u32[]{:S(2)}) collective-permute-start(bf16[8,64,128]{2,1,0:T(8,128)(2,1)S(1)} %get-tuple-element.80), channel_id=1, source_target_pairs={{0,16},{4,20},{8,24},{12,28},{16,0},{20,4},{24,8},{28,12},{1,17},{... | collective-permute-start | bytes 393224 | tf_op jit(solution)/shard_map/ppermute | solution.py:44
  8.6 1.6 collective-permute-start.18
  10.7 3.8 %collective-permute-start.21 = (s32[1,64]{1,0:T(1,128)S(1)}, s32[1,64]{1,0:T(1,128)S(1)}, u32[]{:S(2)}, u32[]{:S(2)}) collective-permute-start(s32[1,64]{1,0:T(1,128)S(1)} %copy-done.7), channel_id=1, source_target_pairs={{0,20},{4,16},{8,28},{12,24},{16,4},{20,0},{24,12},{28,8},{1,21},{... | collective-permute-start | bytes 776 | tf_op jit(solution)/shard_map/ppermute | solution.py:44
  15.8 2.4 %collective-permute-start.23 = (s32[1,64]{1,0:T(1,128)S(1)}, s32[1,64]{1,0:T(1,128)S(1)}, u32[]{:S(2)}, u32[]{:S(2)}) collective-permute-start(s32[1,64]{1,0:T(1,128)S(1)} %copy-done.7), channel_id=1, source_target_pairs={{0,28},{4,24},{8,20},{12,16},{16,12},{20,8},{24,4},{28,0},{1,29},{... | collective-permute-start | bytes 776 | tf_op jit(solution)/shard_map/ppermute | solution.py:44
  19.8 2.3 collective-permute-done.23.refs_7_
  22.1 3.4 %gather.1 = (bf16[144,512]{1,0:T(8,128)(2,1)S(1)}, bf16[144,512]{1,0:T(8,128)(2,1)S(1)}, bf16[144,512]{1,0:T(8,128)(2,1)S(1)}, bf16[144,512]{1,0:T(8,128)(2,1)S(...) custom-call(s32[2]{0:T(128)S(1)} %pad_add_fusion.ids, ...), custom_call_target="tpu_custom_call" | custom-call | tf_op jit(solution)/shard_map/gather/pallas_call | solution.py:23
  25.5 2.9 %collective-permute-start.31 = (bf16[144,512]{1,0:T(8,128)(2,1)S(1)}, bf16[144,512]{1,0:T(8,128)(2,1)S(1)}, u32[]{:S(2)}, u32[]{:S(2)}) collective-permute-start(bf16[144,512]{1,0:T(8,128)(2,1)S(1)} %get-tuple-element.103), channel_id=1, source_target_pairs={{0,20},{4,16},{8,28},{12,24},{16,4},{20,0},{24,12},{28,8},{1,21},{... | collective-permute-start | bytes 442376 | tf_op jit(solution)/shard_map/ppermute | solution.py:44
  29.4 2.5 %collective-permute-start.32 = (bf16[144,512]{1,0:T(8,128)(2,1)S(1)}, bf16[144,512]{1,0:T(8,128)(2,1)S(1)}, u32[]{:S(2)}, u32[]{:S(2)}) collective-permute-start(bf16[144,512]{1,0:T(8,128)(2,1)S(1)} %get-tuple-element.104), channel_id=1, source_target_pairs={{0,24},{4,28},{8,16},{12,20},{16,8},{20,12},{24,0},{28,4},{1,25},{... | collective-permute-start | bytes 442376 | tf_op jit(solution)/shard_map/ppermute | solution.py:44
  33.2 18.8 %collective-permute-done.4.refs_5_ = bf16[8,64,128]{2,1,0:T(8,128)(2,1)S(1)} collective-permute-done((bf16[8,64,128]{2,1,0:T(8,128)(2,1)S(1)}, bf16[8,64,128]{2,1,0:T(8,128)(2,1)S(1)}, u32[]{:S(2)}, u32[]{:S(2)}) %collective-permute-start.4) | collective-permute-done | bytes 131104 | tf_op jit(solution)/shard_map/ppermute | solution.py:44
  52.0 2.0 collective-permute-start.26
  56.9 2.4 %collective-permute-start.6 = (bf16[8,64,128]{2,1,0:T(8,128)(2,1)S(1)}, bf16[8,64,128]{2,1,0:T(8,128)(2,1)S(1)}, u32[]{:S(2)}, u32[]{:S(2)}) collective-permute-start(bf16[8,64,128]{2,1,0:T(8,128)(2,1)S(1)} %get-tuple-element.83), channel_id=1, source_target_pairs={{0,28},{4,24},{8,20},{12,16},{16,12},{20,8},{24,4},{28,0},{1,29},{... | collective-permute-start | bytes 393224 | tf_op jit(solution)/shard_map/ppermute | solution.py:44
  59.3 1.6 collective-permute-start
  60.9 3.6 %collective-permute-done.26 = bf16[144,512]{1,0:T(8,128)(2,1)S(1)} collective-permute-done((bf16[144,512]{1,0:T(8,128)(2,1)S(1)}, bf16[144,512]{1,0:T(8,128)(2,1)S(1)}, u32[]{:S(2)}, u32[]{:S(2)}) %collective-permute-start.26) | collective-permute-done | bytes 147488 | tf_op jit(solution)/shard_map/ppermute | solution.py:44
  64.5 1.7 collective-permute-start.2
  69.8 2.1 collective-permute-done.2.refs_3_
  79.5 1.7 collective-permute-done.15.refs_2_
  82.0 9.1 %collective-permute-done.10.refs_4_ = bf16[8,64,128]{2,1,0:T(8,128)(2,1)S(1)} collective-permute-done((bf16[8,64,128]{2,1,0:T(8,128)(2,1)S(1)}, bf16[8,64,128]{2,1,0:T(8,128)(2,1)S(1)}, u32[]{:S(2)}, u32[]{:S(2)}) %collective-permute-start.10) | collective-permute-done | bytes 131104 | tf_op jit(solution)/shard_map/ppermute | solution.py:44
  91.1 2.1 collective-permute-start.13
  95.3 3.6 %collective-permute-done.13.refs_7_ = bf16[8,64,128]{2,1,0:T(8,128)(2,1)S(1)} collective-permute-done((bf16[8,64,128]{2,1,0:T(8,128)(2,1)S(1)}, bf16[8,64,128]{2,1,0:T(8,128)(2,1)S(1)}, u32[]{:S(2)}, u32[]{:S(2)}) %collective-permute-start.13) | collective-permute-done | bytes 131104 | tf_op jit(solution)/shard_map/ppermute | solution.py:44
  98.9 1.6 collective-permute-done.7.refs_1_
  101.1 4.8 %collective-permute-done.8.refs_2_ = bf16[8,80,128]{2,1,0:T(8,128)(2,1)S(1)} collective-permute-done((bf16[8,80,128]{2,1,0:T(8,128)(2,1)S(1)}, bf16[8,80,128]{2,1,0:T(8,128)(2,1)S(1)}, u32[]{:S(2)}, u32[]{:S(2)}) %collective-permute-start.8) | collective-permute-done | bytes 163872 | tf_op jit(solution)/shard_map/ppermute | solution.py:44
  107.0 5.1 %collective-permute-done.9.refs_3_ = bf16[8,80,128]{2,1,0:T(8,128)(2,1)S(1)} collective-permute-done((bf16[8,80,128]{2,1,0:T(8,128)(2,1)S(1)}, bf16[8,80,128]{2,1,0:T(8,128)(2,1)S(1)}, u32[]{:S(2)}, u32[]{:S(2)}) %collective-permute-start.9) | collective-permute-done | bytes 163872 | tf_op jit(solution)/shard_map/ppermute | solution.py:44
  114.5 3.6 %collective-permute-done.16.refs_3_ = bf16[8,16,512]{2,1,0:T(8,128)(2,1)S(1)} collective-permute-done((bf16[8,16,512]{2,1,0:T(8,128)(2,1)S(1)}, bf16[8,16,512]{2,1,0:T(8,128)(2,1)S(1)}, u32[]{:S(2)}, u32[]{:S(2)}) %collective-permute-start.16) | collective-permute-done | bytes 131104 | tf_op jit(solution)/shard_map/ppermute | solution.py:44
  119.9 1.7 collective-permute-start.42
  121.7 9.5 %forward.1 = (bf16[640,2048]{1,0:T(8,128)(2,1)}, bf16[640,2048]{1,0:T(8,128)(2,1)}, bf16[512,2048]{1,0:T(8,128)(2,1)}, bf16[512,2048]{1,0:T(8,128)(2,1)}, bf16[8...) custom-call(s32[2]{0:T(128)S(1)} %pad_add_fusion.ids, ...), custom_call_target="tpu_custom_call" | custom-call | tf_op jit(solution)/shard_map/forward/pallas_call | solution.py:23
  132.5 1.7 copy-done.2
  134.2 1.6 copy-done.3
  135.8 6.3 %backward_far.1 = (bf16[2,144,2048]{2,1,0:T(8,128)(2,1)S(1)}, bf16[2,144,2048]{2,1,0:T(8,128)(2,1)S(1)}, f32[512,576]{1,0:T(8,128)S(1)}) custom-call(s32[2]{0:T(128)S(1)} %pad_add_fusion.ids, bf16[32,16,64]{2,1,0:T(8,128)(2,1)S(1)} %bitcast.30, f32[512,512]{1,0:T(8,128)S(1)} %copy-done, bf16[640,2048]{1,0:T(8,128)(2,1)S(1)} %copy-done.2, ...), custom_call_target="tpu_custom_call" | custom-call | tf_op jit(solution)/shard_map/backward_far/pallas_call | solution.py:23
  142.1 6.3 %backward_near.1 = (bf16[2,144,2048]{2,1,0:T(8,128)(2,1)S(1)}, bf16[2,144,2048]{2,1,0:T(8,128)(2,1)S(1)}, bf16[8,16,512]{2,1,0:T(8,128)(2,1)S(1)}, bf16[8,16,512...) custom-call(s32[2]{0:T(128)S(1)} %pad_add_fusion.ids, ...), custom_call_target="tpu_custom_call" | custom-call | tf_op jit(solution)/shard_map/backward_near/pallas_call | solution.py:23
  149.0 2.3 collective-permute-done.49.got
  155.6 18.5 %collective-permute-done.58.got = bf16[144,1024]{1,0:T(8,128)(2,1)S(1)} collective-permute-done((bf16[144,1024]{1,0:T(8,128)(2,1)S(1)}, bf16[144,1024]{1,0:T(8,128)(2,1)S(1)}, u32[]{:S(2)}, u32[]{:S(2)}) %collective-permute-start.58) | collective-permute-done | bytes 294944 | tf_op jit(solution)/shard_map/ppermute | solution.py:44
  174.2 1.6 collective-permute-start.59
  175.8 2.3 collective-permute-start.60
  179.8 1.8 collective-permute-start.56
  184.4 9.3 %collective-permute-start.52 = (bf16[144,512]{1,0:T(8,128)(2,1)S(1)}, bf16[144,512]{1,0:T(8,128)(2,1)S(1)}, u32[]{:S(2)}, u32[]{:S(2)}) collective-permute-start(bf16[144,512]{1,0:T(8,128)(2,1)S(1)} %get-tuple-element.137), channel_id=1, source_target_pairs={{0,8},{4,12},{8,0},{12,4},{16,24},{20,28},{24,16},{28,20},{1,9},{5... | collective-permute-start | bytes 442376 | tf_op jit(solution)/shard_map/ppermute | solution.py:44
  193.8 4.4 %collective-permute-start.53 = (bf16[144,512]{1,0:T(8,128)(2,1)S(1)}, bf16[144,512]{1,0:T(8,128)(2,1)S(1)}, u32[]{:S(2)}, u32[]{:S(2)}) collective-permute-start(bf16[144,512]{1,0:T(8,128)(2,1)S(1)} %get-tuple-element.138), channel_id=1, source_target_pairs={{0,12},{4,8},{8,4},{12,0},{16,28},{20,24},{24,20},{28,16},{1,13},{... | collective-permute-start | bytes 442376 | tf_op jit(solution)/shard_map/ppermute | solution.py:44
  199.2 2.2 collective-permute-done.57.refs_13_
  201.4 1.8 collective-permute-done.52.refs_10_
  203.3 1.9 collective-permute-done.53.refs_11_
  205.1 2.2 scatter.1.refs_0_
  210.1 2.3 collective-permute-start.45
  212.4 1.8 collective-permute-done.62.refs_2_
  216.7 1.6 collective-permute-start.39
  218.4 1.7 collective-permute-done.37.refs_1_
  220.1 2.2 collective-permute-done.38.refs_2_
  222.3 1.8 collective-permute-done.39.refs_3_
  226.6 1.7 collective-permute-start.48
  233.7 2.1 assemble.1
  (134 shorter events, 57.4 us)
Async XLA Ops:
  3.0 28.9 %collective-permute-start.3 = (bf16[8,64,128]{2,1,0:T(8,128)(2,1)S(1)}, bf16[8,64,128]{2,1,0:T(8,128)(2,1)S(1)}, u32[]{:S(2)}, u32[]{:S(2)}) collective-permute-start(bf16[8,64,128]{2,1,0:T(8,128)(2,1)S(1)} %get-tuple-element.80), channel_id=1, source_target_pairs={{0,16},{4,20},{8,24},{12,28},{16,0},{20,4},{24,8},{28,12},{1,17},{... | collective-permute-start | bytes 393224 | tf_op jit(solution)/shard_map/ppermute | solution.py:44
  10.6 7.7 %collective-permute-start.20 = (s32[1,64]{1,0:T(1,128)S(1)}, s32[1,64]{1,0:T(1,128)S(1)}, u32[]{:S(2)}, u32[]{:S(2)}) collective-permute-start(s32[1,64]{1,0:T(1,128)S(1)} %copy-done.7), channel_id=1, source_target_pairs={{0,16},{4,20},{8,24},{12,28},{16,0},{20,4},{24,8},{28,12},{1,17},{... | collective-permute-start | bytes 776 | tf_op jit(solution)/shard_map/ppermute | solution.py:44
  10.7 7.6 %collective-permute-start.21 = (s32[1,64]{1,0:T(1,128)S(1)}, s32[1,64]{1,0:T(1,128)S(1)}, u32[]{:S(2)}, u32[]{:S(2)}) collective-permute-start(s32[1,64]{1,0:T(1,128)S(1)} %copy-done.7), channel_id=1, source_target_pairs={{0,20},{4,16},{8,28},{12,24},{16,4},{20,0},{24,12},{28,8},{1,21},{... | collective-permute-start | bytes 776 | tf_op jit(solution)/shard_map/ppermute | solution.py:44
  15.8 6.2 %collective-permute-start.23 = (s32[1,64]{1,0:T(1,128)S(1)}, s32[1,64]{1,0:T(1,128)S(1)}, u32[]{:S(2)}, u32[]{:S(2)}) collective-permute-start(s32[1,64]{1,0:T(1,128)S(1)} %copy-done.7), channel_id=1, source_target_pairs={{0,28},{4,24},{8,20},{12,16},{16,12},{20,8},{24,4},{28,0},{1,29},{... | collective-permute-start | bytes 776 | tf_op jit(solution)/shard_map/ppermute | solution.py:44
  25.4 26.5 %collective-permute-start.30 = (bf16[144,512]{1,0:T(8,128)(2,1)S(1)}, bf16[144,512]{1,0:T(8,128)(2,1)S(1)}, u32[]{:S(2)}, u32[]{:S(2)}) collective-permute-start(bf16[144,512]{1,0:T(8,128)(2,1)S(1)} %get-tuple-element.102), channel_id=1, source_target_pairs={{0,16},{4,20},{8,24},{12,28},{16,0},{20,4},{24,8},{28,12},{1,17},{... | collective-permute-start | bytes 442376 | tf_op jit(solution)/shard_map/ppermute | solution.py:44
  25.5 28.4 %collective-permute-start.31 = (bf16[144,512]{1,0:T(8,128)(2,1)S(1)}, bf16[144,512]{1,0:T(8,128)(2,1)S(1)}, u32[]{:S(2)}, u32[]{:S(2)}) collective-permute-start(bf16[144,512]{1,0:T(8,128)(2,1)S(1)} %get-tuple-element.103), channel_id=1, source_target_pairs={{0,20},{4,16},{8,28},{12,24},{16,4},{20,0},{24,12},{28,8},{1,21},{... | collective-permute-start | bytes 442376 | tf_op jit(solution)/shard_map/ppermute | solution.py:44
  28.4 23.6 %collective-permute-start.4 = (bf16[8,64,128]{2,1,0:T(8,128)(2,1)S(1)}, bf16[8,64,128]{2,1,0:T(8,128)(2,1)S(1)}, u32[]{:S(2)}, u32[]{:S(2)}) collective-permute-start(bf16[8,64,128]{2,1,0:T(8,128)(2,1)S(1)} %get-tuple-element.81), channel_id=1, source_target_pairs={{0,20},{4,16},{8,28},{12,24},{16,4},{20,0},{24,12},{28,8},{1,21},{... | collective-permute-start | bytes 393224 | tf_op jit(solution)/shard_map/ppermute | solution.py:44
  29.4 26.1 %collective-permute-start.32 = (bf16[144,512]{1,0:T(8,128)(2,1)S(1)}, bf16[144,512]{1,0:T(8,128)(2,1)S(1)}, u32[]{:S(2)}, u32[]{:S(2)}) collective-permute-start(bf16[144,512]{1,0:T(8,128)(2,1)S(1)} %get-tuple-element.104), channel_id=1, source_target_pairs={{0,24},{4,28},{8,16},{12,20},{16,8},{20,12},{24,0},{28,4},{1,25},{... | collective-permute-start | bytes 442376 | tf_op jit(solution)/shard_map/ppermute | solution.py:44
  31.9 25.0 %collective-permute-start.33 = (bf16[144,512]{1,0:T(8,128)(2,1)S(1)}, bf16[144,512]{1,0:T(8,128)(2,1)S(1)}, u32[]{:S(2)}, u32[]{:S(2)}) collective-permute-start(bf16[144,512]{1,0:T(8,128)(2,1)S(1)} %get-tuple-element.105), channel_id=1, source_target_pairs={{0,28},{4,24},{8,20},{12,16},{16,12},{20,8},{24,4},{28,0},{1,29},{... | collective-permute-start | bytes 442376 | tf_op jit(solution)/shard_map/ppermute | solution.py:44
  52.0 7.4 %collective-permute-start.25 = (bf16[144,512]{1,0:T(8,128)(2,1)S(1)}, bf16[144,512]{1,0:T(8,128)(2,1)S(1)}, u32[]{:S(2)}, u32[]{:S(2)}) collective-permute-start(bf16[144,512]{1,0:T(8,128)(2,1)S(1)} %get-tuple-element.100), channel_id=1, source_target_pairs={{0,8},{4,12},{8,0},{12,4},{16,24},{20,28},{24,16},{28,20},{1,9},{5... | collective-permute-start | bytes 442376 | tf_op jit(solution)/shard_map/ppermute | solution.py:44
  52.0 12.5 %collective-permute-start.26 = (bf16[144,512]{1,0:T(8,128)(2,1)S(1)}, bf16[144,512]{1,0:T(8,128)(2,1)S(1)}, u32[]{:S(2)}, u32[]{:S(2)}) collective-permute-start(bf16[144,512]{1,0:T(8,128)(2,1)S(1)} %get-tuple-element.101), channel_id=1, source_target_pairs={{0,12},{4,8},{8,4},{12,0},{16,28},{20,24},{24,20},{28,16},{1,13},{... | collective-permute-start | bytes 442376 | tf_op jit(solution)/shard_map/ppermute | solution.py:44
  54.0 10.6 %collective-permute-start.24 = (bf16[144,512]{1,0:T(8,128)(2,1)S(1)}, bf16[144,512]{1,0:T(8,128)(2,1)S(1)}, u32[]{:S(2)}, u32[]{:S(2)}) collective-permute-start(bf16[144,512]{1,0:T(8,128)(2,1)S(1)} %get-tuple-element.99), channel_id=1, source_target_pairs={{0,4},{4,0},{8,12},{12,8},{16,20},{20,16},{24,28},{28,24},{1,5},{5... | collective-permute-start | bytes 442376 | tf_op jit(solution)/shard_map/ppermute | solution.py:44
  55.5 10.8 %collective-permute-start.5 = (bf16[8,64,128]{2,1,0:T(8,128)(2,1)S(1)}, bf16[8,64,128]{2,1,0:T(8,128)(2,1)S(1)}, u32[]{:S(2)}, u32[]{:S(2)}) collective-permute-start(bf16[8,64,128]{2,1,0:T(8,128)(2,1)S(1)} %get-tuple-element.82), channel_id=1, source_target_pairs={{0,24},{4,28},{8,16},{12,20},{16,8},{20,12},{24,0},{28,4},{1,25},{... | collective-permute-start | bytes 393224 | tf_op jit(solution)/shard_map/ppermute | solution.py:44
  56.9 11.0 %collective-permute-start.6 = (bf16[8,64,128]{2,1,0:T(8,128)(2,1)S(1)}, bf16[8,64,128]{2,1,0:T(8,128)(2,1)S(1)}, u32[]{:S(2)}, u32[]{:S(2)}) collective-permute-start(bf16[8,64,128]{2,1,0:T(8,128)(2,1)S(1)} %get-tuple-element.83), channel_id=1, source_target_pairs={{0,28},{4,24},{8,20},{12,16},{16,12},{20,8},{24,4},{28,0},{1,29},{... | collective-permute-start | bytes 393224 | tf_op jit(solution)/shard_map/ppermute | solution.py:44
  59.3 9.1 %collective-permute-start = (bf16[8,80,128]{2,1,0:T(8,128)(2,1)S(1)}, bf16[8,80,128]{2,1,0:T(8,128)(2,1)S(1)}, u32[]{:S(2)}, u32[]{:S(2)}) collective-permute-start(bf16[8,80,128]{2,1,0:T(8,128)(2,1)S(1)} %get-tuple-element.77), channel_id=1, source_target_pairs={{0,4},{4,0},{8,12},{12,8},{16,20},{20,16},{24,28},{28,24},{1,5},{5... | collective-permute-start | bytes 491528 | tf_op jit(solution)/shard_map/ppermute | solution.py:44
  64.5 7.4 %collective-permute-start.2 = (bf16[8,80,128]{2,1,0:T(8,128)(2,1)S(1)}, bf16[8,80,128]{2,1,0:T(8,128)(2,1)S(1)}, u32[]{:S(2)}, u32[]{:S(2)}) collective-permute-start(bf16[8,80,128]{2,1,0:T(8,128)(2,1)S(1)} %get-tuple-element.79), channel_id=1, source_target_pairs={{0,12},{4,8},{8,4},{12,0},{16,28},{20,24},{24,20},{28,16},{1,13},{... | collective-permute-start | bytes 491528 | tf_op jit(solution)/shard_map/ppermute | solution.py:44
  66.3 34.3 %collective-permute-start.35 = (bf16[4,144,512]{2,1,0:T(8,128)(2,1)S(1)}, bf16[4,144,512]{2,1,0:T(8,128)(2,1)S(1)}, u32[]{:S(2)}, u32[]{:S(2)}) collective-permute-start(bf16[4,144,512]{2,1,0:T(8,128)(2,1)S(1)} %pad_maximum_fusion.1.refs_8_), channel_id=1, source_target_pairs={{0,2},{1,3},{2,0},{3,1},{4,6},{5,7},{6,4},{7,5},{8,10},{9,11},{10,... | collective-permute-start | bytes 1769480 | tf_op jit(solution)/shard_map/ppermute | solution.py:44
  67.8 32.8 %collective-permute-start.28 = (bf16[4,144,512]{2,1,0:T(8,128)(2,1)S(1)}, bf16[4,144,512]{2,1,0:T(8,128)(2,1)S(1)}, u32[]{:S(2)}, u32[]{:S(2)}) collective-permute-start(bf16[4,144,512]{2,1,0:T(8,128)(2,1)S(1)} %pad_maximum_fusion.refs_4_), channel_id=1, source_target_pairs={{0,2},{1,3},{2,0},{3,1},{4,6},{5,7},{6,4},{7,5},{8,10},{9,11},{10,... | collective-permute-start | bytes 1769480 | tf_op jit(solution)/shard_map/ppermute | solution.py:44
  74.3 6.8 %collective-permute-start.15 = (bf16[8,16,512]{2,1,0:T(8,128)(2,1)S(1)}, bf16[8,16,512]{2,1,0:T(8,128)(2,1)S(1)}, u32[]{:S(2)}, u32[]{:S(2)}) collective-permute-start(bf16[8,16,512]{2,1,0:T(8,128)(2,1)S(1)} %get-tuple-element.96), channel_id=1, source_target_pairs={{0,8},{4,12},{8,0},{12,4},{16,24},{20,28},{24,16},{28,20},{1,9},{5... | collective-permute-start | bytes 393224 | tf_op jit(solution)/shard_map/ppermute | solution.py:44
  76.1 14.9 %collective-permute-start.10 = (bf16[8,64,128]{2,1,0:T(8,128)(2,1)S(1)}, bf16[8,64,128]{2,1,0:T(8,128)(2,1)S(1)}, u32[]{:S(2)}, u32[]{:S(2)}) collective-permute-start(bf16[8,64,128]{2,1,0:T(8,128)(2,1)S(1)} %get-tuple-element.89), channel_id=1, source_target_pairs={{0,16},{4,20},{8,24},{12,28},{16,0},{20,4},{24,8},{28,12},{1,17},{... | collective-permute-start | bytes 393224 | tf_op jit(solution)/shard_map/ppermute | solution.py:44
  78.0 15.9 %collective-permute-start.11 = (bf16[8,64,128]{2,1,0:T(8,128)(2,1)S(1)}, bf16[8,64,128]{2,1,0:T(8,128)(2,1)S(1)}, u32[]{:S(2)}, u32[]{:S(2)}) collective-permute-start(bf16[8,64,128]{2,1,0:T(8,128)(2,1)S(1)} %get-tuple-element.90), channel_id=1, source_target_pairs={{0,20},{4,16},{8,28},{12,24},{16,4},{20,0},{24,12},{28,8},{1,21},{... | collective-permute-start | bytes 393224 | tf_op jit(solution)/shard_map/ppermute | solution.py:44
  81.2 14.2 %collective-permute-start.12 = (bf16[8,64,128]{2,1,0:T(8,128)(2,1)S(1)}, bf16[8,64,128]{2,1,0:T(8,128)(2,1)S(1)}, u32[]{:S(2)}, u32[]{:S(2)}) collective-permute-start(bf16[8,64,128]{2,1,0:T(8,128)(2,1)S(1)} %get-tuple-element.91), channel_id=1, source_target_pairs={{0,24},{4,28},{8,16},{12,20},{16,8},{20,12},{24,0},{28,4},{1,25},{... | collective-permute-start | bytes 393224 | tf_op jit(solution)/shard_map/ppermute | solution.py:44
  91.1 7.9 %collective-permute-start.13 = (bf16[8,64,128]{2,1,0:T(8,128)(2,1)S(1)}, bf16[8,64,128]{2,1,0:T(8,128)(2,1)S(1)}, u32[]{:S(2)}, u32[]{:S(2)}) collective-permute-start(bf16[8,64,128]{2,1,0:T(8,128)(2,1)S(1)} %get-tuple-element.92), channel_id=1, source_target_pairs={{0,28},{4,24},{8,20},{12,16},{16,12},{20,8},{24,4},{28,0},{1,29},{... | collective-permute-start | bytes 393224 | tf_op jit(solution)/shard_map/ppermute | solution.py:44
  93.9 6.7 %collective-permute-start.7 = (bf16[8,80,128]{2,1,0:T(8,128)(2,1)S(1)}, bf16[8,80,128]{2,1,0:T(8,128)(2,1)S(1)}, u32[]{:S(2)}, u32[]{:S(2)}) collective-permute-start(bf16[8,80,128]{2,1,0:T(8,128)(2,1)S(1)} %get-tuple-element.86), channel_id=1, source_target_pairs={{0,4},{4,0},{8,12},{12,8},{16,20},{20,16},{24,28},{28,24},{1,5},{5... | collective-permute-start | bytes 491528 | tf_op jit(solution)/shard_map/ppermute | solution.py:44
  95.3 23.4 %collective-permute-start.34 = (bf16[4,144,512]{2,1,0:T(8,128)(2,1)S(1)}, bf16[4,144,512]{2,1,0:T(8,128)(2,1)S(1)}, u32[]{:S(2)}, u32[]{:S(2)}) collective-permute-start(bf16[4,144,512]{2,1,0:T(8,128)(2,1)S(1)} %pad_maximum_fusion.1.refs_8_), channel_id=1, source_target_pairs={{0,1},{1,0},{2,3},{3,2},{4,5},{5,4},{6,7},{7,6},{8,9},{9,8},{10,11... | collective-permute-start | bytes 1769480 | tf_op jit(solution)/shard_map/ppermute | solution.py:44
  98.9 20.9 %collective-permute-start.27 = (bf16[4,144,512]{2,1,0:T(8,128)(2,1)S(1)}, bf16[4,144,512]{2,1,0:T(8,128)(2,1)S(1)}, u32[]{:S(2)}, u32[]{:S(2)}) collective-permute-start(bf16[4,144,512]{2,1,0:T(8,128)(2,1)S(1)} %pad_maximum_fusion.refs_4_), channel_id=1, source_target_pairs={{0,1},{1,0},{2,3},{3,2},{4,5},{5,4},{6,7},{7,6},{8,9},{9,8},{10,11... | collective-permute-start | bytes 1769480 | tf_op jit(solution)/shard_map/ppermute | solution.py:44
  100.6 21.1 %collective-permute-start.36 = (bf16[4,144,512]{2,1,0:T(8,128)(2,1)S(1)}, bf16[4,144,512]{2,1,0:T(8,128)(2,1)S(1)}, u32[]{:S(2)}, u32[]{:S(2)}) collective-permute-start(bf16[4,144,512]{2,1,0:T(8,128)(2,1)S(1)} %collective-permute-done.35.refs_10_), channel_id=1, source_target_pairs={{0,1},{1,0},{2,3},{3,2},{4,5},{5,4},{6,7},{7,6},{8,9},{9,8},{10,11... | collective-permute-start | bytes 1769480 | tf_op jit(solution)/shard_map/ppermute | solution.py:44
  100.6 21.1 %collective-permute-start.29 = (bf16[4,144,512]{2,1,0:T(8,128)(2,1)S(1)}, bf16[4,144,512]{2,1,0:T(8,128)(2,1)S(1)}, u32[]{:S(2)}, u32[]{:S(2)}) collective-permute-start(bf16[4,144,512]{2,1,0:T(8,128)(2,1)S(1)} %collective-permute-done.28.refs_6_), channel_id=1, source_target_pairs={{0,1},{1,0},{2,3},{3,2},{4,5},{5,4},{6,7},{7,6},{8,9},{9,8},{10,11... | collective-permute-start | bytes 1769480 | tf_op jit(solution)/shard_map/ppermute | solution.py:44
  105.9 6.2 %collective-permute-start.9 = (bf16[8,80,128]{2,1,0:T(8,128)(2,1)S(1)}, bf16[8,80,128]{2,1,0:T(8,128)(2,1)S(1)}, u32[]{:S(2)}, u32[]{:S(2)}) collective-permute-start(bf16[8,80,128]{2,1,0:T(8,128)(2,1)S(1)} %get-tuple-element.88), channel_id=1, source_target_pairs={{0,12},{4,8},{8,4},{12,0},{16,28},{20,24},{24,20},{28,16},{1,13},{... | collective-permute-start | bytes 491528 | tf_op jit(solution)/shard_map/ppermute | solution.py:44
  118.1 13.1 %collective-permute-start.40 = (bf16[8,16,512]{2,1,0:T(8,128)(2,1)S(1)}, bf16[8,16,512]{2,1,0:T(8,128)(2,1)S(1)}, u32[]{:S(2)}, u32[]{:S(2)}) collective-permute-start(bf16[8,16,512]{2,1,0:T(8,128)(2,1)S(1)} %get-tuple-element.114), channel_id=1, source_target_pairs={{0,4},{4,0},{8,12},{12,8},{16,20},{20,16},{24,28},{28,24},{1,5},{5... | collective-permute-start | bytes 393224 | tf_op jit(solution)/shard_map/ppermute | solution.py:44
  118.7 12.5 %collective-permute-start.41 = (bf16[8,16,512]{2,1,0:T(8,128)(2,1)S(1)}, bf16[8,16,512]{2,1,0:T(8,128)(2,1)S(1)}, u32[]{:S(2)}, u32[]{:S(2)}) collective-permute-start(bf16[8,16,512]{2,1,0:T(8,128)(2,1)S(1)} %get-tuple-element.115), channel_id=1, source_target_pairs={{0,8},{4,12},{8,0},{12,4},{16,24},{20,28},{24,16},{28,20},{1,9},{5... | collective-permute-start | bytes 393224 | tf_op jit(solution)/shard_map/ppermute | solution.py:44
  119.9 11.4 %collective-permute-start.42 = (bf16[8,16,512]{2,1,0:T(8,128)(2,1)S(1)}, bf16[8,16,512]{2,1,0:T(8,128)(2,1)S(1)}, u32[]{:S(2)}, u32[]{:S(2)}) collective-permute-start(bf16[8,16,512]{2,1,0:T(8,128)(2,1)S(1)} %get-tuple-element.116), channel_id=1, source_target_pairs={{0,12},{4,8},{8,4},{12,0},{16,28},{20,24},{24,20},{28,16},{1,13},{... | collective-permute-start | bytes 393224 | tf_op jit(solution)/shard_map/ppermute | solution.py:44
  151.6 31.2 %collective-permute-start.50 = (bf16[144,2048]{1,0:T(8,128)(2,1)S(1)}, bf16[144,2048]{1,0:T(8,128)(2,1)S(1)}, u32[]{:S(2)}, u32[]{:S(2)}) collective-permute-start(bf16[144,2048]{1,0:T(8,128)(2,1)S(1)} %get-tuple-element.134), channel_id=1, source_target_pairs={{0,2},{1,3},{2,0},{3,1},{4,6},{5,7},{6,4},{7,5},{8,10},{9,11},{10,... | collective-permute-start | bytes 1769480 | tf_op jit(solution)/shard_map/ppermute | solution.py:44
  153.5 20.7 %collective-permute-start.58 = (bf16[144,1024]{1,0:T(8,128)(2,1)S(1)}, bf16[144,1024]{1,0:T(8,128)(2,1)S(1)}, u32[]{:S(2)}, u32[]{:S(2)}) collective-permute-start(bf16[144,1024]{1,0:T(8,128)(2,1)S(1)} %get-tuple-element.145), channel_id=1, source_target_pairs={{0,2},{1,3},{2,0},{3,1},{4,6},{5,7},{6,4},{7,5},{8,10},{9,11},{10,... | collective-permute-start | bytes 884744 | tf_op jit(solution)/shard_map/ppermute | solution.py:44
  154.9 24.8 %collective-permute-start.55 = (bf16[144,1024]{1,0:T(8,128)(2,1)S(1)}, bf16[144,1024]{1,0:T(8,128)(2,1)S(1)}, u32[]{:S(2)}, u32[]{:S(2)}) collective-permute-start(bf16[144,1024]{1,0:T(8,128)(2,1)S(1)} %get-tuple-element.142), channel_id=1, source_target_pairs={{0,2},{1,3},{2,0},{3,1},{4,6},{5,7},{6,4},{7,5},{8,10},{9,11},{10,... | collective-permute-start | bytes 884744 | tf_op jit(solution)/shard_map/ppermute | solution.py:44
  174.2 10.2 %collective-permute-start.59 = (bf16[144,512]{1,0:T(8,128)(2,1)S(1)}, bf16[144,512]{1,0:T(8,128)(2,1)S(1)}, u32[]{:S(2)}, u32[]{:S(2)}) collective-permute-start(bf16[144,512]{1,0:T(8,128)(2,1)S(1)} %get-tuple-element.146), channel_id=1, source_target_pairs={{0,24},{4,28},{8,16},{12,20},{16,8},{20,12},{24,0},{28,4},{1,25},{... | collective-permute-start | bytes 442376 | tf_op jit(solution)/shard_map/ppermute | solution.py:44
  175.8 17.9 %collective-permute-start.60 = (bf16[144,512]{1,0:T(8,128)(2,1)S(1)}, bf16[144,512]{1,0:T(8,128)(2,1)S(1)}, u32[]{:S(2)}, u32[]{:S(2)}) collective-permute-start(bf16[144,512]{1,0:T(8,128)(2,1)S(1)} %get-tuple-element.147), channel_id=1, source_target_pairs={{0,28},{4,24},{8,20},{12,16},{16,12},{20,8},{24,4},{28,0},{1,29},{... | collective-permute-start | bytes 442376 | tf_op jit(solution)/shard_map/ppermute | solution.py:44
  179.8 19.5 %collective-permute-start.56 = (bf16[144,512]{1,0:T(8,128)(2,1)S(1)}, bf16[144,512]{1,0:T(8,128)(2,1)S(1)}, u32[]{:S(2)}, u32[]{:S(2)}) collective-permute-start(bf16[144,512]{1,0:T(8,128)(2,1)S(1)} %get-tuple-element.143), channel_id=1, source_target_pairs={{0,16},{4,20},{8,24},{12,28},{16,0},{20,4},{24,8},{28,12},{1,17},{... | collective-permute-start | bytes 442376 | tf_op jit(solution)/shard_map/ppermute | solution.py:44
  181.5 19.9 %collective-permute-start.57 = (bf16[144,512]{1,0:T(8,128)(2,1)S(1)}, bf16[144,512]{1,0:T(8,128)(2,1)S(1)}, u32[]{:S(2)}, u32[]{:S(2)}) collective-permute-start(bf16[144,512]{1,0:T(8,128)(2,1)S(1)} %get-tuple-element.144), channel_id=1, source_target_pairs={{0,20},{4,16},{8,28},{12,24},{16,4},{20,0},{24,12},{28,8},{1,21},{... | collective-permute-start | bytes 442376 | tf_op jit(solution)/shard_map/ppermute | solution.py:44
  182.9 18.5 %collective-permute-start.51 = (bf16[144,512]{1,0:T(8,128)(2,1)S(1)}, bf16[144,512]{1,0:T(8,128)(2,1)S(1)}, u32[]{:S(2)}, u32[]{:S(2)}) collective-permute-start(bf16[144,512]{1,0:T(8,128)(2,1)S(1)} %get-tuple-element.136), channel_id=1, source_target_pairs={{0,4},{4,0},{8,12},{12,8},{16,20},{20,16},{24,28},{28,24},{1,5},{5... | collective-permute-start | bytes 442376 | tf_op jit(solution)/shard_map/ppermute | solution.py:44
  184.4 18.8 %collective-permute-start.52 = (bf16[144,512]{1,0:T(8,128)(2,1)S(1)}, bf16[144,512]{1,0:T(8,128)(2,1)S(1)}, u32[]{:S(2)}, u32[]{:S(2)}) collective-permute-start(bf16[144,512]{1,0:T(8,128)(2,1)S(1)} %get-tuple-element.137), channel_id=1, source_target_pairs={{0,8},{4,12},{8,0},{12,4},{16,24},{20,28},{24,16},{28,20},{1,9},{5... | collective-permute-start | bytes 442376 | tf_op jit(solution)/shard_map/ppermute | solution.py:44
  193.8 11.4 %collective-permute-start.53 = (bf16[144,512]{1,0:T(8,128)(2,1)S(1)}, bf16[144,512]{1,0:T(8,128)(2,1)S(1)}, u32[]{:S(2)}, u32[]{:S(2)}) collective-permute-start(bf16[144,512]{1,0:T(8,128)(2,1)S(1)} %get-tuple-element.138), channel_id=1, source_target_pairs={{0,12},{4,8},{8,4},{12,0},{16,28},{20,24},{24,20},{28,16},{1,13},{... | collective-permute-start | bytes 442376 | tf_op jit(solution)/shard_map/ppermute | solution.py:44
  207.3 6.8 %collective-permute-start.62 = (bf16[144,1024]{1,0:T(8,128)(2,1)S(1)}, bf16[144,1024]{1,0:T(8,128)(2,1)S(1)}, u32[]{:S(2)}, u32[]{:S(2)}) collective-permute-start(bf16[144,1024]{1,0:T(8,128)(2,1)S(1)} %scatter.1.refs_0_), channel_id=1, source_target_pairs={{0,2},{1,3},{2,0},{3,1},{4,6},{5,7},{6,4},{7,5},{8,10},{9,11},{10,... | collective-permute-start | bytes 884744 | tf_op jit(solution)/shard_map/ppermute | solution.py:44
  210.1 6.7 %collective-permute-start.45 = (bf16[8,16,512]{2,1,0:T(8,128)(2,1)S(1)}, bf16[8,16,512]{2,1,0:T(8,128)(2,1)S(1)}, u32[]{:S(2)}, u32[]{:S(2)}) collective-permute-start(bf16[8,16,512]{2,1,0:T(8,128)(2,1)S(1)} %get-tuple-element.123), channel_id=1, source_target_pairs={{0,12},{4,8},{8,4},{12,0},{16,28},{20,24},{24,20},{28,16},{1,13},{... | collective-permute-start | bytes 393224 | tf_op jit(solution)/shard_map/ppermute | solution.py:44
  212.4 21.4 %collective-permute-start.61 = (bf16[144,1024]{1,0:T(8,128)(2,1)S(1)}, bf16[144,1024]{1,0:T(8,128)(2,1)S(1)}, u32[]{:S(2)}, u32[]{:S(2)}) collective-permute-start(bf16[144,1024]{1,0:T(8,128)(2,1)S(1)} %scatter.1.refs_0_), channel_id=1, source_target_pairs={{0,1},{1,0},{2,3},{3,2},{4,5},{5,4},{6,7},{7,6},{8,9},{9,8},{10,11... | collective-permute-start | bytes 884744 | tf_op jit(solution)/shard_map/ppermute | solution.py:44
  214.2 19.6 %collective-permute-start.63 = (bf16[144,1024]{1,0:T(8,128)(2,1)S(1)}, bf16[144,1024]{1,0:T(8,128)(2,1)S(1)}, u32[]{:S(2)}, u32[]{:S(2)}) collective-permute-start(bf16[144,1024]{1,0:T(8,128)(2,1)S(1)} %collective-permute-done.62.refs_2_), channel_id=1, source_target_pairs={{0,1},{1,0},{2,3},{3,2},{4,5},{5,4},{6,7},{7,6},{8,9},{9,8},{10,11... | collective-permute-start | bytes 884744 | tf_op jit(solution)/shard_map/ppermute | solution.py:44
  216.0 6.4 %collective-permute-start.38 = (bf16[8,16,512]{2,1,0:T(8,128)(2,1)S(1)}, bf16[8,16,512]{2,1,0:T(8,128)(2,1)S(1)}, u32[]{:S(2)}, u32[]{:S(2)}) collective-permute-start(bf16[8,16,512]{2,1,0:T(8,128)(2,1)S(1)} %get-tuple-element.108), channel_id=1, source_target_pairs={{0,8},{4,12},{8,0},{12,4},{16,24},{20,28},{24,16},{28,20},{1,9},{5... | collective-permute-start | bytes 393224 | tf_op jit(solution)/shard_map/ppermute | solution.py:44
  216.7 7.4 %collective-permute-start.39 = (bf16[8,16,512]{2,1,0:T(8,128)(2,1)S(1)}, bf16[8,16,512]{2,1,0:T(8,128)(2,1)S(1)}, u32[]{:S(2)}, u32[]{:S(2)}) collective-permute-start(bf16[8,16,512]{2,1,0:T(8,128)(2,1)S(1)} %get-tuple-element.109), channel_id=1, source_target_pairs={{0,12},{4,8},{8,4},{12,0},{16,28},{20,24},{24,20},{28,16},{1,13},{... | collective-permute-start | bytes 393224 | tf_op jit(solution)/shard_map/ppermute | solution.py:44
  (28 other events, 233.3 us)
